TPU v7x, 128 devices: a whole 4x4x4 slice. The times are simulated.
128 devices in a mesh: lat: 8 (over x, y_hi), lon: 16 (over y_lo, z, core).
Axes of the slice: x: 4, y: 4 (y_hi: 2, y_lo: 2; y = y_hi * 2 + y_lo), z: 4, core: 2. Of those that a mesh axis runs over, the one named last changes fastest.
Arguments:
- var_tokens: bfloat16 [64, 384, 8, 1024], P('lat', 'lon'), may hold values from -6 to 6
- ocean_mask: int32 [64, 384, 2], P('lat', 'lon'), may hold values from 0 to 1, as said below
- land_mask: int32 [64, 384, 2], P('lat', 'lon'), may hold values from 0 to 1, as said below
- move_plan: int32 [8, 16, 2], P('lat', 'lon'), may hold values from -1 to 7, as said below
- agg_query: bfloat16 [1024], replicated, may hold values from -6 to 6
- agg_key: bfloat16 [1024, 1024], replicated, may hold values from -0.1875 to 0.1875
- agg_value: bfloat16 [1024, 1024], replicated, may hold values from -0.1875 to 0.1875
- agg_out: bfloat16 [1024, 1024], replicated, may hold values from -0.1875 to 0.1875
- norm_gain: bfloat16 [1024], replicated, may hold values from 0.5 to 1.5
- win_query: bfloat16 [1024, 1024], replicated, may hold values from -0.1875 to 0.1875
- win_key: bfloat16 [1024, 1024], replicated, may hold values from -0.1875 to 0.1875
- win_value: bfloat16 [1024, 1024], replicated, may hold values from -0.1875 to 0.1875
- win_out: bfloat16 [1024, 1024], replicated, may hold values from -0.1875 to 0.1875
- out_cotangent: bfloat16 [64, 384, 1024], P('lat', 'lon'), may hold values from -6 to 6
Outputs:
- layer_out: bfloat16 [64, 384, 1024], P('lat', 'lon')
- token_grad: bfloat16 [80, 384, 8, 1024], P('lat', 'lon')
Inputs may be any that keep to these rules, and one draw needn't show every extreme that they name: `ocean_mask`: 0 on land patches; present ocean variables on ocean patches. `land_mask`: 0 on ocean patches; present land variables on land patches. `move_plan`: entry 0 names a row of the device's 8 patch rows handed to the next lon index (wrapping), entry 1 one handed to the previous; -1 names none; the two entries differ unless -1.
All inputs are finite; a program needn't handle non-finite values.
Results may differ from a plain program's by a relative error of at most 0.023.
Values may be sent and summed in bfloat16 or wider, within the bound.
A program may use at most 128 MiB of HBM per device.

v0:
```python
import functools

import jax
import jax.numpy as jnp
from jax import lax
from jax.experimental import pallas as pl
from jax.experimental.pallas import tpu as pltpu
from jax.sharding import PartitionSpec as P

MESH = pl.DeviceIdType.MESH
HEADS = 16
WIN = 8
EPS = 1e-06
F32 = jnp.float32
BF16 = jnp.bfloat16

D = 1024
HD = D // HEADS
V = 8
PLAT = 8
PLON = 24
N = PLAT * PLON
ROW = PLON * V
LANES = 128
WIDE = 256
PACK = D + 2 * LANES
HALF = N // 2
EDGE = 16
SIDE = 80


def iota(shape, dim):
    return lax.broadcasted_iota(jnp.int32, shape, dim)


def one_hot(mask, dtype=BF16):
    return jnp.where(mask, 1.0, 0.0).astype(dtype)


def nn(a, b):
    return lax.dot_general(a, b, (((1,), (0,)), ((), ())), preferred_element_type=F32)


def nt(a, b):
    return lax.dot_general(a, b, (((1,), (1,)), ((), ())), preferred_element_type=F32)


def tn(a, b):
    return lax.dot_general(a, b, (((0,), (0,)), ((), ())), preferred_element_type=F32)


def head_rows():
    return one_hot(iota((LANES, D), 0) % HEADS == iota((LANES, D), 1) // HD)


def token_lanes(patches):
    shape = (patches, V, LANES)
    return iota(shape, 2) // HEADS == iota(shape, 1)


def over_tokens(x, op):
    for shift in (HEADS, 2 * HEADS, 4 * HEADS):
        x = op(x, pltpu.roll(x, shift, axis=1))
    return x


def fold_tokens(x, patches):
    x = x.reshape(patches, V, LANES)
    return jnp.sum(jnp.where(token_lanes(patches), x, 0.0), axis=1)


def unfold_tokens(x, patches):
    x = jnp.broadcast_to(x[:, None, :], (patches, V, LANES))
    return jnp.where(token_lanes(patches), x, 0.0).reshape(patches * V, LANES).astype(BF16)


def to_quads():
    n, m = iota((HALF, HALF), 0), iota((HALF, HALF), 1)
    return one_hot(((n % 16) // 4) * PLON + (n // 16) * 4 + n % 4 == m)


def from_quads():
    n, m = iota((HALF, HALF), 1), iota((HALF, HALF), 0)
    return one_hot(((n % 16) // 4) * PLON + (n // 16) * 4 + n % 4 == m)


def front(
    n_lat, n_lon,
    tok_hbm, ocean_ref, land_ref, plan_ref, query_ref, gain_ref,
    key_hbm, value_hbm, out_hbm, wq_hbm, wk_hbm, wv_hbm, wo_hbm, cot_hbm,
    lay_ref, pack_ref, kqt_ref,
    tok, w_key, w_value, w_out, w_q, w_k, w_v, w_o, cot,
    values, probs, mixed, heads,
    h_cot, h_cell, h_lay, h_grad, r_cot, r_cell, r_lay, r_grad,
    normed, b_q, b_k, b_v, b_mixdot, b_mix, d_q, d_k, d_v,
    move_out, move_in,
    load_sem, send_sem, recv_sem,
):
    i, j = lax.axis_index("lat"), lax.axis_index("lon")
    north, south = lax.rem(i + n_lat - 1, n_lat), lax.rem(i + 1, n_lat)
    west, east = lax.rem(j + n_lon - 1, n_lon), lax.rem(j + 1, n_lon)
    to_n, to_s, to_w, to_e = (north, j), (south, j), (i, west), (i, east)
    to_nw, to_se = (north, west), (south, east)

    def load(src, dst, slot):
        return pltpu.make_async_copy(src, dst, load_sem.at[slot])

    loads = [
        load(cot_hbm, cot, 0),
        load(key_hbm, w_key, 1),
        load(tok_hbm.at[pl.ds(HALF * V, HALF * V)], tok.at[pl.ds(HALF * V, HALF * V)], 2),
        load(value_hbm, w_value, 3),
        load(tok_hbm.at[pl.ds(0, HALF * V)], tok.at[pl.ds(0, HALF * V)], 4),
        load(out_hbm, w_out, 5),
        load(wo_hbm, w_o, 6),
        load(wq_hbm, w_q, 7),
        load(wk_hbm, w_k, 8),
        load(wv_hbm, w_v, 9),
    ]
    for k in range(6):
        loads[k].start()

    barrier = pltpu.get_barrier_semaphore()
    for to in (to_n, to_s, to_w, to_e, to_nw, to_se):
        pl.semaphore_signal(barrier, inc=1, device_id=to, device_id_type=MESH)

    heads[...] = head_rows()

    def send(src, dst, to, slot):
        return pltpu.make_async_remote_copy(
            src_ref=src, dst_ref=dst, send_sem=send_sem.at[slot], recv_sem=recv_sem.at[slot],
            device_id=to, device_id_type=MESH,
        )

    def outward(home, region, slot):
        return [
            send(home.at[pl.ds(HALF, SIDE)], region.at[pl.ds(EDGE, SIDE)], to_s, slot),
            send(home.at[pl.ds(HALF + SIDE, EDGE)], region.at[pl.ds(0, EDGE)], to_se, slot + 1),
            send(home.at[pl.ds(SIDE, EDGE)], region.at[pl.ds(HALF, EDGE)], to_e, slot + 2),
        ]

    def inward(region, home, slot):
        return [
            send(region.at[pl.ds(EDGE, SIDE)], home.at[pl.ds(HALF, SIDE)], to_n, slot),
            send(region.at[pl.ds(0, EDGE)], home.at[pl.ds(HALF + SIDE, EDGE)], to_nw, slot + 1),
            send(region.at[pl.ds(HALF, EDGE)], home.at[pl.ds(SIDE, EDGE)], to_w, slot + 2),
        ]

    send_cot = outward(h_cot, r_cot, 0)
    send_cell = outward(h_cell, r_cell, 3)
    send_lay = inward(r_lay, h_lay, 6)
    send_grad = inward(r_grad, h_grad, 9)
    send_move = [
        send(move_out.at[0], move_in.at[0], to_e, 12),
        send(move_out.at[1], move_in.at[1], to_w, 13),
    ]

    loads[0].wait()
    quads = to_quads()
    for half in (1, 0):
        rows = pl.ds(half * HALF, HALF)
        h_cot[rows, :] = nn(quads, cot[rows, :]).astype(BF16)
    r_cot[pl.ds(HALF + EDGE, SIDE), :] = h_cot[pl.ds(0, SIDE), :]
    pl.semaphore_wait(barrier, 6)
    for copy in send_cot:
        copy.start()

    loads[1].wait()
    picked = heads[...] * query_ref[...]
    key_query = nt(picked, w_key[...]) * (1.0 / HD**0.5)
    high = key_query.astype(BF16)
    kqt_ref[0:LANES, :] = high
    kqt_ref[LANES:WIDE, :] = (key_query - high.astype(F32)).astype(BF16)

    for k in range(6, 10):
        loads[k].start()

    lane_token = iota((PLON, LANES), 1) // HEADS

    def live_of(row):
        pick_o = one_hot(iota((2, LANES), 0) + 4 == iota((2, LANES), 1) // HEADS, F32)
        pick_l = one_hot(iota((2, LANES), 0) + 6 == iota((2, LANES), 1) // HEADS, F32)
        there = tn(ocean_ref[row].astype(F32), pick_o) + tn(land_ref[row].astype(F32), pick_l)
        return (lane_token < 4) | (there > 0.5)

    chunk = 2 * PLON
    fold = one_hot(iota((chunk, chunk * V), 1) // V == iota((chunk, chunk * V), 0))

    def aggregate(c):
        first = pl.multiple_of(c * chunk, 16)
        t_rows = pl.ds(pl.multiple_of(c * chunk * V, 16), chunk * V)
        tokens = tok[t_rows, :]
        both = nt(tokens, kqt_ref[...])
        scores = fold_tokens(both[:, :LANES] + both[:, LANES:], chunk)
        live = jnp.concatenate([live_of(c * 2), live_of(c * 2 + 1)], axis=0)
        scores = jnp.where(live, scores, -1e30)
        expo = jnp.exp(scores - over_tokens(scores, jnp.maximum))
        prob = expo / over_tokens(expo, jnp.add)
        probs[pl.ds(first, chunk), :] = prob
        spread = unfold_tokens(prob, chunk)
        for n in range(D // WIDE):
            cols = slice(n * WIDE, (n + 1) * WIDE)
            vals = nn(tokens, w_value[:, cols]).astype(BF16)
            values[t_rows, cols] = vals
            weighted = nn(spread, heads[:, cols]) * vals.astype(F32)
            mixed[pl.ds(first, chunk), cols] = nn(fold, weighted.astype(BF16)).astype(BF16)

    loads[3].wait()
    for half in (1, 0):
        loads[2 if half else 4].wait()

        @pl.loop(2 * half, 2 * half + 2)
        def _(c):
            aggregate(c)

        rows = pl.ds(half * HALF, HALF)
        if half:
            loads[5].wait()
        cells = nn(mixed[rows, :], w_out[...]).astype(BF16)
        h_cell[rows, :] = nn(quads, cells).astype(BF16)
        if half:
            send_cell[0].start()
            send_cell[1].start()
    send_cell[2].start()
    r_cell[pl.ds(HALF + EDGE, SIDE), :] = h_cell[pl.ds(0, SIDE), :]

    for copy in send_cot:
        copy.wait_recv()
    loads[6].wait()
    b_mixdot[...] = nt(r_cot[...], w_o[...]).astype(BF16)

    for copy in send_cell:
        copy.wait_recv()
    wide = r_cell[...].astype(F32)
    scale = lax.rsqrt(jnp.mean(wide * wide, axis=-1, keepdims=True) + EPS)
    normed[...] = (wide * scale * gain_ref[...].astype(F32)).astype(BF16)
    for slot, (weight, out) in enumerate(((w_q, b_q), (w_k, b_k), (w_v, b_v))):
        loads[7 + slot].wait()
        out[...] = nn(normed[...], weight[...]).astype(BF16)

    patches = WIN * WIN
    half_win = patches // 2
    pole = i == 0
    own_head = one_hot(iota((WIDE, WIDE), 0) // patches == iota((WIDE, WIDE), 1) // HD)
    far = (iota((patches, WIDE), 0) < half_win) != (iota((patches, WIDE), 1) % patches < half_win)
    bias = jnp.where(far & pole, -1e30, 0.0)
    lane_head = iota((patches, WIDE), 1) // HD

    def per_head(x):
        return jnp.concatenate([x] * (WIDE // HD), axis=0) * own_head

    def own_blocks(x):
        out = x[0:patches]
        for h in range(1, WIDE // HD):
            out = jnp.where(lane_head == h, x[h * patches : (h + 1) * patches], out)
        return out

    @pl.loop(0, D // WIDE)
    def _(g):
        cols = pl.ds(pl.multiple_of(g * WIDE, WIDE), WIDE)
        for w in range(N // patches):
            upper, lower = pl.ds(w * half_win, half_win), pl.ds(HALF + w * half_win, half_win)

            def get(ref):
                return jnp.concatenate([ref[upper, cols], ref[lower, cols]], axis=0)

            def put(ref, x):
                x = x.astype(BF16)
                ref[upper, cols] = x[:half_win]
                ref[lower, cols] = x[half_win:]

            keys, vals = get(b_k), get(b_v)
            queries = per_head(get(b_q))
            scores = nt(keys, queries) * (1.0 / HD**0.5) + bias
            expo = jnp.exp(scores - jnp.max(scores, axis=0, keepdims=True))
            prob = expo / jnp.sum(expo, axis=0, keepdims=True)
            prob_b = prob.astype(BF16)
            put(b_mix, own_blocks(tn(prob_b, vals)))
            mixdot = per_head(get(b_mixdot))
            d_prob = nt(vals, mixdot)
            inner = jnp.sum(d_prob * prob, axis=0, keepdims=True)
            d_score = (prob * (d_prob - inner) * (1.0 / HD**0.5)).astype(BF16)
            put(d_v, nn(prob_b, mixdot))
            put(d_k, nn(d_score, queries))
            put(d_q, own_blocks(tn(d_score, keys)))

    d_norm = nt(d_q[...], w_q[...]) + nt(d_k[...], w_k[...]) + nt(d_v[...], w_v[...])
    wide = r_cell[...].astype(F32)
    scale = lax.rsqrt(jnp.mean(wide * wide, axis=-1, keepdims=True) + EPS)
    d_unit = d_norm * gain_ref[...].astype(F32)
    along = jnp.mean(wide * d_unit, axis=-1, keepdims=True)
    grad = r_cot[...].astype(F32) + scale * d_unit - wide * (scale * scale * scale * along)
    r_grad[...] = grad.astype(BF16)
    for copy in send_grad:
        copy.start()
    h_grad[pl.ds(0, SIDE), :] = r_grad[pl.ds(HALF + EDGE, SIDE), :]

    result = r_cell[...].astype(F32) + nn(b_mix[...], w_o[...])
    r_lay[...] = result.astype(BF16)
    for copy in send_lay:
        copy.start()
    h_lay[pl.ds(0, SIDE), :] = r_lay[pl.ds(HALF + EDGE, SIDE), :]

    for copy in send_grad:
        copy.wait_recv()
    rows_of = from_quads()
    cell_grad = jnp.concatenate(
        [nn(rows_of, h_grad[0:HALF, :]), nn(rows_of, h_grad[HALF:N, :])], axis=0
    ).astype(BF16)

    def agg_back(grads, prob, values_of, patches):
        d_mixed = nt(grads, w_out[...]).astype(BF16)
        expand = one_hot(iota((patches * V, patches), 0) // V == iota((patches * V, patches), 1))
        d_prob = jnp.zeros((patches * V, LANES), F32)
        for n in range(D // WIDE):
            cols = slice(n * WIDE, (n + 1) * WIDE)
            product = nn(expand, d_mixed[:, cols]) * values_of(cols).astype(F32)
            d_prob += nt(product.astype(BF16), heads[:, cols])
        d_prob = fold_tokens(d_prob, patches)
        d_score = prob * (d_prob - over_tokens(prob * d_prob, jnp.add))
        return d_mixed, d_score

    index = (plan_ref[0, 0], plan_ref[0, 1])
    shape = (2 * PLON, N)
    wanted = jnp.where(
        iota(shape, 0) < PLON,
        jnp.where(index[0] >= 0, index[0] * PLON, -N),
        jnp.where(index[1] >= 0, index[1] * PLON - PLON, -N),
    )
    pick = one_hot(wanted + iota(shape, 0) == iota(shape, 1))
    leaving = nn(pick, cell_grad).astype(BF16)
    prob = nn(pick, probs[...].astype(BF16))

    def row_of(e, cols):
        out = values[0:ROW, cols]
        for r in range(1, PLAT):
            out = jnp.where(e == r, values[r * ROW : (r + 1) * ROW, cols], out)
        return out

    d_mixed, d_score = agg_back(
        leaving,
        prob,
        lambda cols: jnp.concatenate([row_of(e, cols) for e in index], axis=0),
        2 * PLON,
    )
    for k in range(2):
        rows = slice(k * PLON, (k + 1) * PLON)
        pad = jnp.zeros((32 - PLON, PACK), F32)
        block = jnp.concatenate([d_mixed[rows].astype(F32), prob[rows], d_score[rows]], axis=1)
        move_out[k] = jnp.concatenate([block, pad], axis=0).astype(BF16)
        send_move[k].start()

    for r in range(0, PLAT, 2):
        two = 2 * PLON
        d_mixed, d_score = (None, None)
        prob = probs[r * PLON : r * PLON + two, :]
        row = r + iota((two, 1), 0) // PLON
        kept = (row != index[0]) & (row != index[1])
        grads = jnp.where(kept, cell_grad[r * PLON : r * PLON + two].astype(F32), 0.0).astype(BF16)
        d_mixed, d_score = agg_back(
            grads, prob, lambda cols: values[r * ROW : (r + 2) * ROW, cols], two
        )
        block = jnp.concatenate([d_mixed.astype(F32), prob, d_score], axis=1)
        pad = jnp.zeros((32 - PLON, PACK), F32)
        for k in range(2):
            rows = slice(k * PLON, (k + 1) * PLON)
            pack_ref[r + k] = jnp.concatenate([block[rows], pad], axis=0).astype(BF16)

    for copy in send_lay:
        copy.wait_recv()
    for half in (0, 1):
        rows = slice(half * HALF, (half + 1) * HALF)
        lay_ref[rows, :] = nn(rows_of, h_lay[rows, :]).astype(BF16)
    for copy in send_move:
        copy.wait_recv()
    for k in range(2):
        pack_ref[PLAT + k] = move_in[k]
    for copy in send_cot + send_cell + send_lay + send_grad + send_move:
        copy.wait_send()


def back(pack_ref, value_ref, kqt_ref, lay_ref, grad_ref, lay_out_ref, heads):
    @pl.when(pl.program_id(0) == 0)
    def _():
        heads[...] = head_rows()
        lay_out_ref[...] = lay_ref[...]

    expand = one_hot(iota((ROW, 32), 0) // V == iota((ROW, 32), 1))
    for k in range(pack_ref.shape[0]):
        block = pack_ref[k]
        prob = unfold_tokens(block[:PLON, D : D + LANES].astype(F32), PLON)
        d_score = unfold_tokens(block[:PLON, D + LANES :].astype(F32), PLON)
        d_values = nn(prob, heads[...]) * nn(expand, block[:, :D])
        out = nt(d_values.astype(BF16), value_ref[...])
        out += nn(jnp.concatenate([d_score, d_score], axis=1), kqt_ref[...])
        grad_ref[k * ROW : (k + 1) * ROW, :] = out.astype(BF16)


def body(
    n_lat, n_lon,
    var_tokens, ocean_mask, land_mask, move_plan, agg_query, agg_key, agg_value, agg_out,
    norm_gain, win_query, win_key, win_value, win_out, out_cotangent,
):
    anywhere = pl.BlockSpec(memory_space=pl.ANY)
    vmem = pl.BlockSpec(memory_space=pltpu.VMEM)
    smem = pl.BlockSpec(memory_space=pltpu.SMEM)
    weight = pltpu.VMEM((D, D), BF16)
    patch = pltpu.VMEM((N, D), BF16)
    lay, pack, kqt = pl.pallas_call(
        functools.partial(front, n_lat, n_lon),
        out_shape=(
            jax.ShapeDtypeStruct((N, D), BF16),
            jax.ShapeDtypeStruct((PLAT + 2, 32, PACK), BF16),
            jax.ShapeDtypeStruct((WIDE, D), BF16),
        ),
        in_specs=[anywhere, vmem, vmem, smem, vmem, vmem] + [anywhere] * 8,
        out_specs=(vmem, vmem, vmem),
        scratch_shapes=[pltpu.VMEM((N * V, D), BF16)]
        + [weight] * 7
        + [patch, pltpu.VMEM((N * V, D), BF16), pltpu.VMEM((N, LANES), F32), patch]
        + [pltpu.VMEM((LANES, D), BF16)]
        + [patch] * 8
        + [patch] * 9
        + [pltpu.VMEM((2, 32, PACK), BF16)] * 2
        + [
            pltpu.SemaphoreType.DMA((10,)),
            pltpu.SemaphoreType.DMA((14,)),
            pltpu.SemaphoreType.DMA((14,)),
        ],
        compiler_params=pltpu.CompilerParams(
            collective_id=0, has_side_effects=True, vmem_limit_bytes=52 * 1024 * 1024
        ),
        name="front",
    )(
        var_tokens.reshape(N * V, D),
        jnp.transpose(ocean_mask, (0, 2, 1)),
        jnp.transpose(land_mask, (0, 2, 1)),
        move_plan.reshape(1, 2),
        agg_query.reshape(1, D),
        norm_gain.reshape(1, D),
        agg_key, agg_value, agg_out, win_query, win_key, win_value, win_out,
        out_cotangent.reshape(N, D),
    )

    rows = 2
    fixed = lambda shape: pl.BlockSpec(shape, lambda r: (0,) * len(shape))
    token_grad, layer_out = pl.pallas_call(
        back,
        grid=((PLAT + 2) // rows,),
        out_shape=(
            jax.ShapeDtypeStruct(((PLAT + 2) * ROW, D), BF16),
            jax.ShapeDtypeStruct((N, D), BF16),
        ),
        in_specs=[
            pl.BlockSpec((rows, 32, PACK), lambda r: (r, 0, 0)),
            fixed((D, D)),
            fixed((WIDE, D)),
            fixed((N, D)),
        ],
        out_specs=(pl.BlockSpec((rows * ROW, D), lambda r: (r, 0)), fixed((N, D))),
        scratch_shapes=[pltpu.VMEM((LANES, D), BF16)],
        compiler_params=pltpu.CompilerParams(vmem_limit_bytes=32 * 1024 * 1024),
        name="back",
    )(pack, agg_value, kqt, lay)
    return (
        layer_out.reshape(PLAT, PLON, D),
        token_grad.reshape(PLAT + 2, PLON, V, D),
    )


def solution(mesh):
    placed = P("lat", "lon", None)
    return jax.shard_map(
        functools.partial(body, mesh.shape["lat"], mesh.shape["lon"]),
        mesh=mesh,
        in_specs=(P("lat", "lon", None, None), placed, placed, placed) + (P(),) * 9 + (placed,),
        out_specs=(placed, P("lat", "lon", None, None)),
        check_vma=False,
    )
```

profile of v0, /device:TPU:6, one launch (start us, length us, event | category | flops | bytes accessed | tf_op | source)
XLA Modules:
  0.0 68.9 jit_solution(14540887944297996260)
XLA Ops:
  0.6 0.7 reshape.27.query_ref
  1.3 0.7 reshape.28.gain_ref
  2.0 0.0 copy-start.2
  2.0 1.0 %copy-done.2 = bf16[8,24,1024]{2,1,0:T(8,128)(2,1)S(1)} copy-done((bf16[8,24,1024]{2,1,0:T(8,128)(2,1)S(1)}, bf16[8,24,1024]{2,1,0:T(8,128)(2,1)}, u32[]{:S(2)}) %copy-start.2) | copy-done | bytes 393240
  3.0 0.0 copy-start.3
  3.0 0.7 %copy-done.3 = s32[8,24,2]{1,2,0:T(2,128)S(1)} copy-done((s32[8,24,2]{1,2,0:T(2,128)S(1)}, s32[8,24,2]{1,2,0:T(2,128)}, u32[]{:S(2)}) %copy-start.3) | copy-done | bytes 1560
  3.7 0.0 copy-start.4
  3.7 0.7 %copy-done.4 = s32[8,24,2]{1,2,0:T(2,128)S(1)} copy-done((s32[8,24,2]{1,2,0:T(2,128)S(1)}, s32[8,24,2]{1,2,0:T(2,128)}, u32[]{:S(2)}) %copy-start.4) | copy-done | bytes 1560
  4.4 0.0 copy-start.5
  4.4 0.7 copy-done.5
  5.0 0.0 copy-start
  5.1 50.9 %front.1 = (bf16[192,1024]{1,0:T(8,128)(2,1)S(1)}, bf16[10,32,1280]{2,1,0:T(8,128)(2,1)}, bf16[256,1024]{1,0:T(8,128)(2,1)S(1)}) custom-call(bf16[1536,1024]{1,0:T(8,128)(2,1)} %bitcast.11, s32[8,2,24]{2,1,0:T(2,128)S(1)} %bitcast.8, s32[8,2,24]{2,1,0:T(2,128)S(1)} %bitcast.9, s32[1,2]{1,0:T(1,128)S(1)} %bitcast.10, bf16[1,1024]{1,0:T(2,128)(2,1)S(1)} %reshape.27.query_ref, ...), custom_call_target="tpu_custom_call" | custom-call | tf_op jit(solution)/shard_map/front/pallas_call | solution.py:409
  56.0 0.0 copy-done
  56.0 0.0 copy-start.1
  56.0 1.1 %copy-done.1 = bf16[10,32,1280]{2,1,0:T(8,128)(2,1)S(1)} copy-done((bf16[10,32,1280]{2,1,0:T(8,128)(2,1)S(1)}, bf16[10,32,1280]{2,1,0:T(8,128)(2,1)}, u32[]{:S(2)}) %copy-start.1) | copy-done | bytes 819224
  57.2 11.8 %back.1 = (bf16[1920,1024]{1,0:T(8,128)(2,1)}, bf16[192,1024]{1,0:T(8,128)(2,1)}) custom-call(bf16[10,32,1280]{2,1,0:T(8,128)(2,1)S(1)} %copy-done.1, bf16[1024,1024]{1,0:T(8,128)(2,1)S(1)} %copy-done, bf16[256,1024]{1,0:T(8,128)(2,1)S(1)} %get-tuple-element.8.kqt_ref, bf16[192,1024]{1,0:T(8,128)(2,1)S(1)} %get-tuple-element.9.lay_ref), custom_call_target="tpu_custom_call" | custom-call | tf_op jit(solution)/shard_map/back/pallas_call | solution.py:447
Async XLA Ops:
  2.0 1.0 %copy-start.2 = (bf16[8,24,1024]{2,1,0:T(8,128)(2,1)S(1)}, bf16[8,24,1024]{2,1,0:T(8,128)(2,1)}, u32[]{:S(2)}) copy-start(bf16[8,24,1024]{2,1,0:T(8,128)(2,1)} %param.27) | copy-start | bytes 1179652
  3.0 0.7 %copy-start.3 = (s32[8,24,2]{1,2,0:T(2,128)S(1)}, s32[8,24,2]{1,2,0:T(2,128)}, u32[]{:S(2)}) copy-start(s32[8,24,2]{1,2,0:T(2,128)} %param.15) | copy-start | bytes 4612
  3.7 0.7 %copy-start.4 = (s32[8,24,2]{1,2,0:T(2,128)S(1)}, s32[8,24,2]{1,2,0:T(2,128)}, u32[]{:S(2)}) copy-start(s32[8,24,2]{1,2,0:T(2,128)} %param.16) | copy-start | bytes 4612
  4.4 0.7 copy-start.5
  5.0 51.0 %copy-start = (bf16[1024,1024]{1,0:T(8,128)(2,1)S(1)}, bf16[1024,1024]{1,0:T(8,128)(2,1)}, u32[]{:S(2)}) copy-start(bf16[1024,1024]{1,0:T(8,128)(2,1)} %value_ref.1) | copy-start | bytes 6291460
  56.0 1.1 %copy-start.1 = (bf16[10,32,1280]{2,1,0:T(8,128)(2,1)S(1)}, bf16[10,32,1280]{2,1,0:T(8,128)(2,1)}, u32[]{:S(2)}) copy-start(bf16[10,32,1280]{2,1,0:T(8,128)(2,1)} %get-tuple-element.7.pack_ref) | copy-start | bytes 2457604
where the time goes:
time: 69.2 us; the launch traced here: 68.9 us
  Pallas kernels  62.7 us (91%)
  local copies, waits for them, and re-layouts  5.56 us (8%)
    pallas_call x1, Pallas kernels, body(): pl.pallas_call(functools.partial(front, n_lat, n_lon), out_shape=(jax.Sha...  50.9 us
    pallas_call x1, Pallas kernels, body(): pl.pallas_call(back, grid=((PLAT + 2) // rows,), out_shape=(jax.ShapeDtyp...  11.8 us
    unnamed x12, local copies, waits for them, and re-layouts  4.18 us

commit v1 on v0

v1 whole, which is shorter than its diff:
```python
import functools

import jax
import jax.numpy as jnp
from jax import lax
from jax.experimental import pallas as pl
from jax.experimental.pallas import tpu as pltpu
from jax.sharding import PartitionSpec as P

MESH = pl.DeviceIdType.MESH
HEADS = 16
WIN = 8
EPS = 1e-06
F32 = jnp.float32
BF16 = jnp.bfloat16

D = 1024
HD = D // HEADS
V = 8
PLAT = 8
PLON = 24
N = PLAT * PLON
ROW = PLON * V
LANES = 128
WIDE = 256
HALF = N // 2
EDGE = 16
SIDE = 80
GROUP = 32
SPAN = GROUP * V


def iota(shape, dim):
    return lax.broadcasted_iota(jnp.int32, shape, dim)


def one_hot(mask, dtype=BF16):
    return jnp.where(mask, 1.0, 0.0).astype(dtype)


def nn(a, b):
    return lax.dot_general(a, b, (((1,), (0,)), ((), ())), preferred_element_type=F32)


def nt(a, b):
    return lax.dot_general(a, b, (((1,), (1,)), ((), ())), preferred_element_type=F32)


def tn(a, b):
    return lax.dot_general(a, b, (((0,), (0,)), ((), ())), preferred_element_type=F32)


def head_rows():
    return one_hot(iota((HEADS, D), 0) == iota((HEADS, D), 1) // HD)


def stack(x):
    return jnp.concatenate([x[:, k : k + LANES] for k in range(0, x.shape[1], LANES)], axis=0)


def unstack(x):
    return jnp.concatenate([x[k : k + HEADS] for k in range(0, x.shape[0], HEADS)], axis=1)


def over_tokens(x, op):
    lane = iota(x.shape, 1)
    for step in (1, 2, 4):
        other = jnp.where(
            lane & step == 0, pltpu.roll(x, LANES - step, axis=1), pltpu.roll(x, step, axis=1)
        )
        x = op(x, other)
    return x


def to_quads():
    n, m = iota((HALF, HALF), 0), iota((HALF, HALF), 1)
    return one_hot(((n % 16) // 4) * PLON + (n // 16) * 4 + n % 4 == m)


def from_quads():
    n, m = iota((HALF, HALF), 1), iota((HALF, HALF), 0)
    return one_hot(((n % 16) // 4) * PLON + (n // 16) * 4 + n % 4 == m)


def front(
    n_lat, n_lon,
    tok_hbm, ocean_hbm, land_hbm, plan_hbm, query_hbm, gain_hbm,
    key_hbm, value_hbm, out_hbm, wq_hbm, wk_hbm, wv_hbm, wo_hbm, cot_hbm,
    lay_ref, mixdot_ref, probs_ref, scores_ref, kq_ref,
    tok, w_key, w_value, w_out, w_q, w_k, w_v, w_o, cot,
    ocean, land, query, gain, plan,
    values, probs, d_probs, mixed, d_mixed, live,
    h_cot, h_cell, h_lay, h_grad, r_cot, r_cell, r_lay, r_grad,
    normed, b_q, b_k, b_v, b_mixdot, b_mix, d_q, d_k, d_v,
    move_out, move_in, move_out_p, move_in_p,
    load_sem, send_sem, recv_sem,
):
    i, j = lax.axis_index("lat"), lax.axis_index("lon")
    north, south = lax.rem(i + n_lat - 1, n_lat), lax.rem(i + 1, n_lat)
    west, east = lax.rem(j + n_lon - 1, n_lon), lax.rem(j + 1, n_lon)
    to_n, to_s, to_w, to_e = (north, j), (south, j), (i, west), (i, east)
    to_nw, to_se = (north, west), (south, east)

    def load(src, dst, slot):
        return pltpu.make_async_copy(src, dst, load_sem.at[slot])

    upper, lower = pl.ds(0, HALF * V), pl.ds(HALF * V, HALF * V)
    loads = {
        "tok1": load(tok_hbm.at[lower], tok.at[lower], 0),
        "value": load(value_hbm, w_value, 1),
        "key": load(key_hbm, w_key, 2),
        "query": load(query_hbm, query, 3),
        "cot": load(cot_hbm, cot, 4),
        "ocean": load(ocean_hbm, ocean, 5),
        "land": load(land_hbm, land, 6),
        "tok0": load(tok_hbm.at[upper], tok.at[upper], 7),
        "out": load(out_hbm, w_out, 8),
        "wo": load(wo_hbm, w_o, 9),
        "gain": load(gain_hbm, gain, 10),
        "plan": load(plan_hbm, plan, 11),
        "wq": load(wq_hbm, w_q, 12),
        "wk": load(wk_hbm, w_k, 13),
        "wv": load(wv_hbm, w_v, 14),
    }
    early = ("tok1", "value", "key", "query", "cot", "ocean", "land")
    for name in early:
        loads[name].start()

    barrier = pltpu.get_barrier_semaphore()
    for to in (to_n, to_s, to_w, to_e, to_nw, to_se):
        pl.semaphore_signal(barrier, inc=1, device_id=to, device_id_type=MESH)

    def send(src, dst, to, slot):
        return pltpu.make_async_remote_copy(
            src_ref=src, dst_ref=dst, send_sem=send_sem.at[slot], recv_sem=recv_sem.at[slot],
            device_id=to, device_id_type=MESH,
        )

    def outward(home, region, slot):
        return [
            send(home.at[pl.ds(HALF, SIDE)], region.at[pl.ds(EDGE, SIDE)], to_s, slot),
            send(home.at[pl.ds(HALF + SIDE, EDGE)], region.at[pl.ds(0, EDGE)], to_se, slot + 1),
            send(home.at[pl.ds(SIDE, EDGE)], region.at[pl.ds(HALF, EDGE)], to_e, slot + 2),
        ]

    def inward(region, home, slot):
        return [
            send(region.at[pl.ds(EDGE, SIDE)], home.at[pl.ds(HALF, SIDE)], to_n, slot),
            send(region.at[pl.ds(0, EDGE)], home.at[pl.ds(HALF + SIDE, EDGE)], to_nw, slot + 1),
            send(region.at[pl.ds(HALF, EDGE)], home.at[pl.ds(SIDE, EDGE)], to_w, slot + 2),
        ]

    send_cot = outward(h_cot, r_cot, 0)
    send_cell = outward(h_cell, r_cell, 3)
    send_lay = inward(r_lay, h_lay, 6)
    send_grad = inward(r_grad, h_grad, 9)
    send_move = [
        send(move_out.at[0], move_in.at[0], to_e, 12),
        send(move_out.at[1], move_in.at[1], to_w, 13),
        send(move_out_p.at[0], move_in_p.at[0], to_e, 14),
        send(move_out_p.at[1], move_in_p.at[1], to_w, 15),
    ]

    loads["ocean"].wait()
    loads["land"].wait()
    rows16 = [ocean[r] for r in range(PLAT)] + [land[r] for r in range(PLAT)]
    there = jnp.concatenate(rows16, axis=0).astype(F32)
    shape = (PLON, N * V)
    there = nn(there, one_hot((iota(shape, 1) // V) % PLON == iota(shape, 0), F32))
    shape = there.shape
    line, spot = iota(shape, 0), iota(shape, 1)
    mine = ((line // 2) % PLAT == spot // ROW) & (4 + 2 * (line // 16) + line % 2 == spot % V)
    there = nn(jnp.ones((HEADS, 32), F32), jnp.where(mine, there, 0.0))
    live[...] = jnp.where(iota((HEADS, N * V), 1) % V < 4, 1.0, there)

    loads["cot"].wait()
    quads = to_quads()
    for half in (1, 0):
        rows = pl.ds(half * HALF, HALF)
        h_cot[rows, :] = nn(quads, cot[rows, :]).astype(BF16)
    r_cot[pl.ds(HALF + EDGE, SIDE), :] = h_cot[pl.ds(0, SIDE), :]
    pl.semaphore_wait(barrier, 6)
    for copy in send_cot:
        copy.start()

    loads["key"].wait()
    loads["query"].wait()
    picked = head_rows() * query[...][None, :]
    key_query = nt(picked, w_key[...]) * (1.0 / HD**0.5)
    high = key_query.astype(BF16)
    kq_ref[0:HEADS, :] = high
    kq_ref[HEADS : 2 * HEADS, :] = (key_query - high.astype(F32)).astype(BF16)

    loads["tok1"].wait()
    loads["value"].wait()
    for name in loads:
        if name not in early:
            loads[name].start()

    shape = (GROUP, SPAN)
    same_patch = iota(shape, 0) == iota(shape, 1) // V
    lane_head = iota(shape, 1) // HD
    heads_here = WIDE // HD

    for half in (1, 0):
        t_rows = slice(half * HALF * V, (half + 1) * HALF * V)
        if not half:
            loads["tok0"].wait()
        both = nt(kq_ref[...], tok[t_rows, :])
        scores = stack(both[:HEADS] + both[HEADS:])
        scores = jnp.where(stack(live[:, t_rows]) > 0.5, scores, -1e30)
        expo = jnp.exp(scores - over_tokens(scores, jnp.maximum))
        prob = unstack(expo / over_tokens(expo, jnp.add))
        probs[:, t_rows] = prob
        for n in range(D // WIDE):
            cols = slice(n * WIDE, (n + 1) * WIDE)
            vals = nn(tok[t_rows, :], w_value[:, cols]).astype(BF16)
            values[t_rows, cols] = vals
            for g in range(HALF // GROUP):
                span = slice(g * SPAN, (g + 1) * SPAN)
                weigh = [
                    jnp.where(same_patch, prob[h : h + 1, span], 0.0)
                    for h in range(n * heads_here, (n + 1) * heads_here)
                ]
                out = nn(jnp.concatenate(weigh, axis=0).astype(BF16), vals[span])
                pick = out[:GROUP]
                for h in range(1, heads_here):
                    pick = jnp.where(lane_head == h, out[h * GROUP : (h + 1) * GROUP], pick)
                first = half * HALF + g * GROUP
                mixed[first : first + GROUP, cols] = pick.astype(BF16)

        rows = pl.ds(half * HALF, HALF)
        if half:
            loads["out"].wait()
        cells = nn(mixed[rows, :], w_out[...]).astype(BF16)
        h_cell[rows, :] = nn(quads, cells).astype(BF16)
        if half:
            send_cell[0].start()
            send_cell[1].start()
    send_cell[2].start()
    r_cell[pl.ds(HALF + EDGE, SIDE), :] = h_cell[pl.ds(0, SIDE), :]

    for copy in send_cot:
        copy.wait_recv()
    loads["wo"].wait()
    b_mixdot[...] = nt(r_cot[...], w_o[...]).astype(BF16)

    for copy in send_cell:
        copy.wait_recv()
    loads["gain"].wait()
    wide = r_cell[...].astype(F32)
    scale = lax.rsqrt(jnp.mean(wide * wide, axis=-1, keepdims=True) + EPS)
    normed[...] = (wide * scale * gain[...].astype(F32)[None, :]).astype(BF16)
    for name, weight, out in (("wq", w_q, b_q), ("wk", w_k, b_k), ("wv", w_v, b_v)):
        loads[name].wait()
        out[...] = nn(normed[...], weight[...]).astype(BF16)

    patches = WIN * WIN
    half_win = patches // 2
    pole = i == 0
    own_head = one_hot(iota((WIDE, WIDE), 0) // patches == iota((WIDE, WIDE), 1) // HD)
    far = (iota((patches, WIDE), 0) < half_win) != (iota((patches, WIDE), 1) % patches < half_win)
    bias = jnp.where(far & pole, -1e30, 0.0)
    win_head = iota((patches, WIDE), 1) // HD

    def per_head(x):
        return jnp.concatenate([x] * (WIDE // HD), axis=0) * own_head

    def own_blocks(x):
        out = x[0:patches]
        for h in range(1, WIDE // HD):
            out = jnp.where(win_head == h, x[h * patches : (h + 1) * patches], out)
        return out

    @pl.loop(0, D // WIDE)
    def _(g):
        cols = pl.ds(pl.multiple_of(g * WIDE, WIDE), WIDE)
        for w in range(N // patches):
            upper, lower = pl.ds(w * half_win, half_win), pl.ds(HALF + w * half_win, half_win)

            def get(ref):
                return jnp.concatenate([ref[upper, cols], ref[lower, cols]], axis=0)

            def put(ref, x):
                x = x.astype(BF16)
                ref[upper, cols] = x[:half_win]
                ref[lower, cols] = x[half_win:]

            keys, vals = get(b_k), get(b_v)
            queries = per_head(get(b_q))
            scores = nt(keys, queries) * (1.0 / HD**0.5) + bias
            expo = jnp.exp(scores - jnp.max(scores, axis=0, keepdims=True))
            prob = expo / jnp.sum(expo, axis=0, keepdims=True)
            prob_b = prob.astype(BF16)
            put(b_mix, own_blocks(tn(prob_b, vals)))
            mixdot = per_head(get(b_mixdot))
            d_prob = nt(vals, mixdot)
            inner = jnp.sum(d_prob * prob, axis=0, keepdims=True)
            d_score = (prob * (d_prob - inner) * (1.0 / HD**0.5)).astype(BF16)
            put(d_v, nn(prob_b, mixdot))
            put(d_k, nn(d_score, queries))
            put(d_q, own_blocks(tn(d_score, keys)))

    d_norm = nt(d_q[...], w_q[...]) + nt(d_k[...], w_k[...]) + nt(d_v[...], w_v[...])
    wide = r_cell[...].astype(F32)
    scale = lax.rsqrt(jnp.mean(wide * wide, axis=-1, keepdims=True) + EPS)
    d_unit = d_norm * gain[...].astype(F32)[None, :]
    along = jnp.mean(wide * d_unit, axis=-1, keepdims=True)
    grad = r_cot[...].astype(F32) + scale * d_unit - wide * (scale * scale * scale * along)
    r_grad[...] = grad.astype(BF16)
    for copy in send_grad:
        copy.start()
    h_grad[pl.ds(0, SIDE), :] = r_grad[pl.ds(HALF + EDGE, SIDE), :]

    for copy in send_grad:
        copy.wait_recv()
    result = r_cell[...].astype(F32) + nn(b_mix[...], w_o[...])
    r_lay[...] = result.astype(BF16)
    for copy in send_lay:
        copy.start()
    h_lay[pl.ds(0, SIDE), :] = r_lay[pl.ds(HALF + EDGE, SIDE), :]
    rows_of = from_quads()
    cell_grad = jnp.concatenate(
        [nn(rows_of, h_grad[0:HALF, :]), nn(rows_of, h_grad[HALF:N, :])], axis=0
    ).astype(BF16)
    d_mixed[...] = nt(cell_grad, w_out[...]).astype(BF16)
    shape = (heads_here * GROUP, WIDE)
    own_lanes = one_hot(iota(shape, 0) // GROUP == iota(shape, 1) // HD)
    for g in range(N // GROUP):
        rows, t_rows = slice(g * GROUP, (g + 1) * GROUP), slice(g * SPAN, (g + 1) * SPAN)
        for n in range(D // WIDE):
            cols = slice(n * WIDE, (n + 1) * WIDE)
            spread = jnp.concatenate([d_mixed[rows, cols]] * heads_here, axis=0) * own_lanes
            out = nt(spread, values[t_rows, cols])
            for h in range(heads_here):
                part = jnp.where(same_patch, out[h * GROUP : (h + 1) * GROUP], 0.0)
                head = n * heads_here + h
                d_probs[head : head + 1, t_rows] = jnp.sum(part, axis=0, keepdims=True)
    prob, d_prob = stack(probs[...]), stack(d_probs[...])
    d_score = unstack(prob * (d_prob - over_tokens(prob * d_prob, jnp.add)))
    prob = probs[...]

    loads["plan"].wait()
    index = (plan[0, 0], plan[0, 1])
    shape = (PLON, N)
    for k, name in enumerate(index):
        start = jnp.where(name >= 0, name * PLON, -N)
        picked = nn(one_hot(start + iota(shape, 0) == iota(shape, 1)), d_mixed[...])
        pad = jnp.zeros((32 - PLON, D), F32)
        move_out[k] = jnp.concatenate([picked, pad], axis=0).astype(BF16)
        row = jnp.zeros((2 * HEADS, ROW), F32)
        for r in range(PLAT):
            lanes = slice(r * ROW, (r + 1) * ROW)
            here = jnp.concatenate([prob[:, lanes], d_score[:, lanes]], axis=0)
            row = jnp.where(name == r, here, row)
        pad = jnp.zeros((2 * HEADS, WIDE - ROW), F32)
        move_out_p[k] = jnp.concatenate([row, pad], axis=1).astype(BF16)
        send_move[k].start()
        send_move[2 + k].start()

    spot = iota((HEADS, N * V), 1) // ROW
    probs_ref[:, 0 : N * V] = prob.astype(BF16)
    kept = (spot != index[0]) & (spot != index[1])
    scores_ref[:, 0 : N * V] = jnp.where(kept, d_score, 0.0).astype(BF16)
    spot = iota((N, D), 0) // PLON
    kept = (spot != index[0]) & (spot != index[1])
    mixdot_ref[0:N, :] = jnp.where(kept, d_mixed[...].astype(F32), 0.0).astype(BF16)

    for copy in send_lay:
        copy.wait_recv()
    for half in (0, 1):
        rows = slice(half * HALF, (half + 1) * HALF)
        lay_ref[rows, :] = nn(rows_of, h_lay[rows, :]).astype(BF16)
    for copy in send_move:
        copy.wait_recv()
    arrived = [move_in[k].astype(F32)[:PLON] for k in range(2)]
    mixdot_ref[N : N + 2 * PLON, :] = jnp.concatenate(arrived, axis=0).astype(BF16)
    arrived = [move_in_p[k].astype(F32)[:, :ROW] for k in range(2)]
    arrived = jnp.concatenate(arrived, axis=1).astype(BF16)
    probs_ref[:, N * V :] = arrived[:HEADS]
    scores_ref[:, N * V :] = arrived[HEADS:]
    for copy in send_cot + send_cell + send_lay + send_grad + send_move:
        copy.wait_send()


def back(mixdot_ref, probs_ref, scores_ref, value_ref, kq_ref, lay_ref, grad_ref, lay_out_ref, d_values):
    @pl.when(pl.program_id(0) == 0)
    def _():
        lay_out_ref[...] = lay_ref[...]

    patches, tokens = mixdot_ref.shape[0], probs_ref.shape[1]
    expand = one_hot(iota((tokens, patches), 0) // V == iota((tokens, patches), 1))
    heads = head_rows()
    for n in range(D // WIDE):
        cols = slice(n * WIDE, (n + 1) * WIDE)
        wide = tn(probs_ref[...], heads[:, cols]) * nn(expand, mixdot_ref[:, cols])
        d_values[:, cols] = wide.astype(BF16)
    twice = jnp.concatenate([scores_ref[...]] * 2, axis=0)
    for n in range(D // WIDE):
        cols = slice(n * WIDE, (n + 1) * WIDE)
        out = nt(d_values[...], value_ref[cols, :]) + tn(twice, kq_ref[:, cols])
        grad_ref[:, cols] = out.astype(BF16)


def body(
    n_lat, n_lon,
    var_tokens, ocean_mask, land_mask, move_plan, agg_query, agg_key, agg_value, agg_out,
    norm_gain, win_query, win_key, win_value, win_out, out_cotangent,
):
    hbm = pl.BlockSpec(memory_space=pltpu.HBM)
    vmem = pl.BlockSpec(memory_space=pltpu.VMEM)
    weight = pltpu.VMEM((D, D), BF16)
    patch = pltpu.VMEM((N, D), BF16)
    tokens = (PLAT + 2) * ROW
    lay, mixdot, probs, scores, kq = pl.pallas_call(
        functools.partial(front, n_lat, n_lon),
        out_shape=(
            jax.ShapeDtypeStruct((N, D), BF16),
            jax.ShapeDtypeStruct((N + 2 * PLON, D), BF16),
            jax.ShapeDtypeStruct((HEADS, tokens), BF16),
            jax.ShapeDtypeStruct((HEADS, tokens), BF16),
            jax.ShapeDtypeStruct((2 * HEADS, D), BF16),
        ),
        in_specs=[hbm] * 14,
        out_specs=(vmem,) * 5,
        scratch_shapes=[pltpu.VMEM((N * V, D), BF16)]
        + [weight] * 7
        + [patch]
        + [pltpu.VMEM((PLAT, 2, PLON), jnp.int32)] * 2
        + [pltpu.VMEM((D,), BF16)] * 2
        + [pltpu.SMEM((1, 2), jnp.int32)]
        + [pltpu.VMEM((N * V, D), BF16)]
        + [pltpu.VMEM((HEADS, N * V), F32)] * 2
        + [patch] * 2
        + [pltpu.VMEM((HEADS, N * V), F32)]
        + [patch] * 8
        + [patch] * 9
        + [pltpu.VMEM((2, 32, D), BF16)] * 2
        + [pltpu.VMEM((2, 2 * HEADS, WIDE), BF16)] * 2
        + [
            pltpu.SemaphoreType.DMA((15,)),
            pltpu.SemaphoreType.DMA((16,)),
            pltpu.SemaphoreType.DMA((16,)),
        ],
        compiler_params=pltpu.CompilerParams(
            collective_id=0, has_side_effects=True, vmem_limit_bytes=44 * 1024 * 1024
        ),
        name="front",
    )(
        var_tokens.reshape(N * V, D),
        jnp.transpose(ocean_mask, (0, 2, 1)),
        jnp.transpose(land_mask, (0, 2, 1)),
        move_plan.reshape(1, 2),
        agg_query,
        norm_gain,
        agg_key, agg_value, agg_out, win_query, win_key, win_value, win_out,
        out_cotangent.reshape(N, D),
    )

    two = 2 * PLON
    fixed = lambda shape: pl.BlockSpec(shape, lambda r: (0,) * len(shape))
    token_grad, layer_out = pl.pallas_call(
        back,
        grid=(PLAT // 2 + 1,),
        out_shape=(
            jax.ShapeDtypeStruct((tokens, D), BF16),
            jax.ShapeDtypeStruct((N, D), BF16),
        ),
        in_specs=[
            pl.BlockSpec((two, D), lambda r: (r, 0)),
            pl.BlockSpec((HEADS, two * V), lambda r: (0, r)),
            pl.BlockSpec((HEADS, two * V), lambda r: (0, r)),
            fixed((D, D)),
            fixed((2 * HEADS, D)),
            fixed((N, D)),
        ],
        out_specs=(pl.BlockSpec((two * V, D), lambda r: (r, 0)), fixed((N, D))),
        scratch_shapes=[pltpu.VMEM((two * V, D), BF16)],
        compiler_params=pltpu.CompilerParams(vmem_limit_bytes=24 * 1024 * 1024),
        name="back",
    )(mixdot, probs, scores, agg_value, kq, lay)
    return (
        layer_out.reshape(PLAT, PLON, D),
        token_grad.reshape(PLAT + 2, PLON, V, D),
    )


def solution(mesh):
    placed = P("lat", "lon", None)
    return jax.shard_map(
        functools.partial(body, mesh.shape["lat"], mesh.shape["lon"]),
        mesh=mesh,
        in_specs=(P("lat", "lon", None, None), placed, placed, placed) + (P(),) * 9 + (placed,),
        out_specs=(placed, P("lat", "lon", None, None)),
        check_vma=False,
    )
```

time: 69.2 us -> 68.4 us (0.988); the launches traced: 68.9 us -> 67.2 us
  Pallas kernels: 62.7 us -> 55.8 us
  local copies, waits for them, and re-layouts: 5.56 us -> 10.8 us
    unnamed x12 -> x20, local copies, waits for them, and re-layouts: 4.18 us -> 10.8 us
    pallas_call x1, Pallas kernels: 50.9 us -> 46.7 us  [body(): pl.pallas_call(functools.partial(front, n_lat, n_lon), out_shape=(jax.Sha...]
    pallas_call x1, Pallas kernels: 11.8 us -> 9.07 us  [body(): pl.pallas_call(back, grid=(PLAT // 2 + 1,), out_shape=(jax.ShapeDtypeStru...]
    reshape x2 -> x0, local copies, waits for them, and re-layouts: 1.37 us -> none  [the longest x1 0.69 us: body(): agg_query.reshape(1, D)]
where the time goes in v1:
time: 68.4 us; the launch traced here: 67.2 us
  Pallas kernels  55.8 us (82%)
  local copies, waits for them, and re-layouts  10.8 us (16%)
    pallas_call x1, Pallas kernels, body(): pl.pallas_call(functools.partial(front, n_lat, n_lon), out_shape=(jax.Sha...  46.7 us
    unnamed x20, local copies, waits for them, and re-layouts  10.8 us
    pallas_call x1, Pallas kernels, body(): pl.pallas_call(back, grid=(PLAT // 2 + 1,), out_shape=(jax.ShapeDtypeStru...  9.07 us

profile of v1, /device:TPU:6, one launch (start us, length us, event | category | flops | bytes accessed | tf_op | source)
XLA Modules:
  0.0 67.2 jit_solution(8244377467770781190)
XLA Ops:
  0.6 0.0 copy-start
  0.6 1.6 %copy-done = bf16[1024,1024]{1,0:T(8,128)(2,1)S(1)} copy-done((bf16[1024,1024]{1,0:T(8,128)(2,1)S(1)}, bf16[1024,1024]{1,0:T(8,128)(2,1)}, u32[]{:S(2)}) %copy-start) | copy-done | bytes 2097176
  2.2 0.0 copy-start.1
  2.2 1.6 %copy-done.1 = bf16[1024,1024]{1,0:T(8,128)(2,1)S(1)} copy-done((bf16[1024,1024]{1,0:T(8,128)(2,1)S(1)}, bf16[1024,1024]{1,0:T(8,128)(2,1)}, u32[]{:S(2)}) %copy-start.1) | copy-done | bytes 2097176
  3.8 0.0 copy-start.2
  3.8 1.6 %copy-done.2 = bf16[1024,1024]{1,0:T(8,128)(2,1)S(1)} copy-done((bf16[1024,1024]{1,0:T(8,128)(2,1)S(1)}, bf16[1024,1024]{1,0:T(8,128)(2,1)}, u32[]{:S(2)}) %copy-start.2) | copy-done | bytes 2097176
  5.4 0.0 copy-start.3
  5.4 1.6 %copy-done.3 = bf16[1024,1024]{1,0:T(8,128)(2,1)S(1)} copy-done((bf16[1024,1024]{1,0:T(8,128)(2,1)S(1)}, bf16[1024,1024]{1,0:T(8,128)(2,1)}, u32[]{:S(2)}) %copy-start.3) | copy-done | bytes 2097176
  7.0 0.0 copy-start.4
  7.0 1.0 %copy-done.4 = bf16[8,24,1024]{2,1,0:T(8,128)(2,1)S(1)} copy-done((bf16[8,24,1024]{2,1,0:T(8,128)(2,1)S(1)}, bf16[8,24,1024]{2,1,0:T(8,128)(2,1)}, u32[]{:S(2)}) %copy-start.4) | copy-done | bytes 393240
  8.0 0.0 copy-start.5
  8.0 0.7 %copy-done.5 = s32[8,24,2]{1,2,0:T(2,128)S(1)} copy-done((s32[8,24,2]{1,2,0:T(2,128)S(1)}, s32[8,24,2]{1,2,0:T(2,128)}, u32[]{:S(2)}) %copy-start.5) | copy-done | bytes 1560
  8.7 0.0 copy-start.6
  8.7 0.7 %copy-done.6 = s32[8,24,2]{1,2,0:T(2,128)S(1)} copy-done((s32[8,24,2]{1,2,0:T(2,128)S(1)}, s32[8,24,2]{1,2,0:T(2,128)}, u32[]{:S(2)}) %copy-start.6) | copy-done | bytes 1560
  9.4 0.0 copy-start.7
  9.4 0.7 %copy-done.7 = bf16[1024]{0:T(1024)(128)(2,1)S(1)} copy-done((bf16[1024]{0:T(1024)(128)(2,1)S(1)}, bf16[1024]{0:T(1024)(128)(2,1)}, u32[]{:S(2)}) %copy-start.7) | copy-done | bytes 2072
  10.1 0.0 copy-start.8
  10.1 0.7 %copy-done.8 = bf16[1024]{0:T(1024)(128)(2,1)S(1)} copy-done((bf16[1024]{0:T(1024)(128)(2,1)S(1)}, bf16[1024]{0:T(1024)(128)(2,1)}, u32[]{:S(2)}) %copy-start.8) | copy-done | bytes 2072
  10.8 0.0 copy-start.9
  10.8 0.7 copy-done.9
  11.4 46.7 %front.1 = (bf16[192,1024]{1,0:T(8,128)(2,1)S(1)}, bf16[240,1024]{1,0:T(8,128)(2,1)S(1)}, bf16[16,1920]{1,0:T(8,128)(2,1)S(1)}, bf16[16,1920]{1,0:T(8,128)(2,1)S(1)}, bf16[32,1024]{1,0:T(8,128)(2,1)S(1)}) custom-call(bf16[1536,1024]{1,0:T(8,128)(2,1)} %bitcast.11, s32[8,2,24]{2,1,0:T(2,128)S(1)} %bitcast.8, s32[8,2,24]{2,1,0:T(2,128)S(1)} %bitcast.9, ...), custom_call_target="tpu_custom_call" | custom-call | tf_op jit(solution)/shard_map/front/pallas_call | solution.py:415
  58.1 9.1 %back.1 = (bf16[1920,1024]{1,0:T(8,128)(2,1)}, bf16[192,1024]{1,0:T(8,128)(2,1)}) custom-call(bf16[240,1024]{1,0:T(8,128)(2,1)S(1)} %get-tuple-element.9.mixdot_ref, bf16[16,1920]{1,0:T(8,128)(2,1)S(1)} %get-tuple-element.10.probs_ref, bf16[16,1920]{1,0:T(8,128)(2,1)S(1)} %get-tuple-element.11.scores_ref, bf16[1024,1024]{1,0:T(8,128)(2,1)S(1)} %copy-done, ...), custom_call_target="tpu_custom_call" | custom-call | tf_op jit(solution)/shard_map/back/pallas_call | solution.py:462
Async XLA Ops:
  0.6 1.6 %copy-start = (bf16[1024,1024]{1,0:T(8,128)(2,1)S(1)}, bf16[1024,1024]{1,0:T(8,128)(2,1)}, u32[]{:S(2)}) copy-start(bf16[1024,1024]{1,0:T(8,128)(2,1)} %value_ref.1) | copy-start | bytes 6291460
  2.2 1.6 %copy-start.1 = (bf16[1024,1024]{1,0:T(8,128)(2,1)S(1)}, bf16[1024,1024]{1,0:T(8,128)(2,1)}, u32[]{:S(2)}) copy-start(bf16[1024,1024]{1,0:T(8,128)(2,1)} %key_hbm.1) | copy-start | bytes 6291460
  3.8 1.6 %copy-start.2 = (bf16[1024,1024]{1,0:T(8,128)(2,1)S(1)}, bf16[1024,1024]{1,0:T(8,128)(2,1)}, u32[]{:S(2)}) copy-start(bf16[1024,1024]{1,0:T(8,128)(2,1)} %out_hbm.1) | copy-start | bytes 6291460
  5.4 1.6 %copy-start.3 = (bf16[1024,1024]{1,0:T(8,128)(2,1)S(1)}, bf16[1024,1024]{1,0:T(8,128)(2,1)}, u32[]{:S(2)}) copy-start(bf16[1024,1024]{1,0:T(8,128)(2,1)} %wq_hbm.1) | copy-start | bytes 6291460
  7.0 1.0 %copy-start.4 = (bf16[8,24,1024]{2,1,0:T(8,128)(2,1)S(1)}, bf16[8,24,1024]{2,1,0:T(8,128)(2,1)}, u32[]{:S(2)}) copy-start(bf16[8,24,1024]{2,1,0:T(8,128)(2,1)} %param.27) | copy-start | bytes 1179652
  8.0 0.7 %copy-start.5 = (s32[8,24,2]{1,2,0:T(2,128)S(1)}, s32[8,24,2]{1,2,0:T(2,128)}, u32[]{:S(2)}) copy-start(s32[8,24,2]{1,2,0:T(2,128)} %param.15) | copy-start | bytes 4612
  8.7 0.7 %copy-start.6 = (s32[8,24,2]{1,2,0:T(2,128)S(1)}, s32[8,24,2]{1,2,0:T(2,128)}, u32[]{:S(2)}) copy-start(s32[8,24,2]{1,2,0:T(2,128)} %param.16) | copy-start | bytes 4612
  9.4 0.7 %copy-start.7 = (bf16[1024]{0:T(1024)(128)(2,1)S(1)}, bf16[1024]{0:T(1024)(128)(2,1)}, u32[]{:S(2)}) copy-start(bf16[1024]{0:T(1024)(128)(2,1)} %query_hbm.1) | copy-start | bytes 6148
  10.1 0.7 %copy-start.8 = (bf16[1024]{0:T(1024)(128)(2,1)S(1)}, bf16[1024]{0:T(1024)(128)(2,1)}, u32[]{:S(2)}) copy-start(bf16[1024]{0:T(1024)(128)(2,1)} %gain_hbm.1) | copy-start | bytes 6148
  10.8 0.7 copy-start.9

commit v2 on v1

--- a/solution.py
+++ b/solution.py
@@ -28,6 +28,8 @@
 SIDE = 80
 GROUP = 32
 SPAN = GROUP * V
+DEEP = D + LANES
+TOKENS = (PLAT + 2) * ROW
 
 
 def iota(shape, dim):
@@ -82,14 +84,14 @@
     return one_hot(((n % 16) // 4) * PLON + (n // 16) * 4 + n % 4 == m)
 
 
-def front(
+def layer(
     n_lat, n_lon,
     tok_hbm, ocean_hbm, land_hbm, plan_hbm, query_hbm, gain_hbm,
     key_hbm, value_hbm, out_hbm, wq_hbm, wk_hbm, wv_hbm, wo_hbm, cot_hbm,
-    lay_ref, mixdot_ref, probs_ref, scores_ref, kq_ref,
+    lay_ref, grad_hbm,
     tok, w_key, w_value, w_out, w_q, w_k, w_v, w_o, cot,
     ocean, land, query, gain, plan,
-    values, probs, d_probs, mixed, d_mixed, live,
+    values, d_values, grad_out, probs, d_probs, mixed, d_mixed, live, kq,
     h_cot, h_cell, h_lay, h_grad, r_cot, r_cell, r_lay, r_grad,
     normed, b_q, b_k, b_v, b_mixdot, b_mix, d_q, d_k, d_v,
     move_out, move_in, move_out_p, move_in_p,
@@ -107,7 +109,7 @@
     upper, lower = pl.ds(0, HALF * V), pl.ds(HALF * V, HALF * V)
     loads = {
         "tok1": load(tok_hbm.at[lower], tok.at[lower], 0),
-        "value": load(value_hbm, w_value, 1),
+        "value": load(value_hbm, w_value.at[:, pl.ds(0, D)], 1),
         "key": load(key_hbm, w_key, 2),
         "query": load(query_hbm, query, 3),
         "cot": load(cot_hbm, cot, 4),
@@ -179,23 +181,25 @@
         rows = pl.ds(half * HALF, HALF)
         h_cot[rows, :] = nn(quads, cot[rows, :]).astype(BF16)
     r_cot[pl.ds(HALF + EDGE, SIDE), :] = h_cot[pl.ds(0, SIDE), :]
-    pl.semaphore_wait(barrier, 6)
-    for copy in send_cot:
-        copy.start()
 
     loads["key"].wait()
     loads["query"].wait()
     picked = head_rows() * query[...][None, :]
     key_query = nt(picked, w_key[...]) * (1.0 / HD**0.5)
     high = key_query.astype(BF16)
-    kq_ref[0:HEADS, :] = high
-    kq_ref[HEADS : 2 * HEADS, :] = (key_query - high.astype(F32)).astype(BF16)
+    low = key_query - high.astype(F32)
+    both = jnp.concatenate([high.astype(F32), low, jnp.zeros((LANES - 2 * HEADS, D), F32)], axis=0)
+    kq[...] = both[: 2 * HEADS].astype(BF16)
+    w_value[:, D:DEEP] = both.T.astype(BF16)
 
     loads["tok1"].wait()
     loads["value"].wait()
     for name in loads:
         if name not in early:
             loads[name].start()
+    pl.semaphore_wait(barrier, 6)
+    for copy in send_cot:
+        copy.start()
 
     shape = (GROUP, SPAN)
     same_patch = iota(shape, 0) == iota(shape, 1) // V
@@ -206,7 +210,7 @@
         t_rows = slice(half * HALF * V, (half + 1) * HALF * V)
         if not half:
             loads["tok0"].wait()
-        both = nt(kq_ref[...], tok[t_rows, :])
+        both = nt(kq[...], tok[t_rows, :])
         scores = stack(both[:HEADS] + both[HEADS:])
         scores = jnp.where(stack(live[:, t_rows]) > 0.5, scores, -1e30)
         expo = jnp.exp(scores - over_tokens(scores, jnp.maximum))
@@ -272,9 +276,8 @@
             out = jnp.where(win_head == h, x[h * patches : (h + 1) * patches], out)
         return out
 
-    @pl.loop(0, D // WIDE)
-    def _(g):
-        cols = pl.ds(pl.multiple_of(g * WIDE, WIDE), WIDE)
+    for g in range(D // WIDE):
+        cols = slice(g * WIDE, (g + 1) * WIDE)
         for w in range(N // patches):
             upper, lower = pl.ds(w * half_win, half_win), pl.ds(HALF + w * half_win, half_win)
 
@@ -312,36 +315,75 @@
         copy.start()
     h_grad[pl.ds(0, SIDE), :] = r_grad[pl.ds(HALF + EDGE, SIDE), :]
 
-    for copy in send_grad:
-        copy.wait_recv()
     result = r_cell[...].astype(F32) + nn(b_mix[...], w_o[...])
     r_lay[...] = result.astype(BF16)
+    h_lay[pl.ds(0, SIDE), :] = r_lay[pl.ds(HALF + EDGE, SIDE), :]
+    rows_of = from_quads()
+    shape = (heads_here * GROUP, WIDE)
+    own_lanes = one_hot(iota(shape, 0) // GROUP == iota(shape, 1) // HD)
+    two = 2 * PLON
+    expand = one_hot(iota((two * V, two), 0) // V == iota((two * V, two), 1))
+    heads = head_rows()
+    loads["plan"].wait()
+    index = (plan[0, 0], plan[0, 1])
+
+    def agg_back(half):
+        rows, t_rows = pl.ds(half * HALF, HALF), slice(half * HALF * V, (half + 1) * HALF * V)
+        cell_grad = nn(rows_of, h_grad[rows, :]).astype(BF16)
+        d_mixed[rows, :] = nt(cell_grad, w_out[...]).astype(BF16)
+        for g in range(half * HALF // GROUP, (half + 1) * HALF // GROUP):
+            group, span = slice(g * GROUP, (g + 1) * GROUP), slice(g * SPAN, (g + 1) * SPAN)
+            for n in range(D // WIDE):
+                cols = slice(n * WIDE, (n + 1) * WIDE)
+                spread = jnp.concatenate([d_mixed[group, cols]] * heads_here, axis=0) * own_lanes
+                out = nt(spread, values[span, cols])
+                for h in range(heads_here):
+                    part = jnp.where(same_patch, out[h * GROUP : (h + 1) * GROUP], 0.0)
+                    head = n * heads_here + h
+                    d_probs[head : head + 1, span] = jnp.sum(part, axis=0, keepdims=True)
+        prob, d_prob = stack(probs[:, t_rows]), stack(d_probs[:, t_rows])
+        d_probs[:, t_rows] = unstack(prob * (d_prob - over_tokens(prob * d_prob, jnp.add)))
+
+    def token_back(first, prob, d_score, here):
+        t_rows = pl.ds(first * V, two * V)
+        for n in range(D // WIDE):
+            cols = slice(n * WIDE, (n + 1) * WIDE)
+            wide = tn(prob, heads[:, cols]) * nn(expand, here[:, cols])
+            d_values[t_rows, cols] = wide.astype(BF16)
+        pad = jnp.zeros((LANES - 2 * HEADS, two * V), F32)
+        d_values[t_rows, D:DEEP] = jnp.concatenate([d_score, d_score, pad], axis=0).T.astype(BF16)
+
+    def multiply(first, count, slot):
+        t_rows = pl.ds(first * V, count * V)
+        for n in range(D // WIDE):
+            cols = slice(n * WIDE, (n + 1) * WIDE)
+            grad_out[t_rows, cols] = nt(d_values[t_rows, :], w_value[cols, :]).astype(BF16)
+        store = pltpu.make_async_copy(grad_out.at[t_rows], grad_hbm.at[t_rows], load_sem.at[slot])
+        store.start()
+        return store
+
+    def half_back(half):
+        for c in range(2 * half, 2 * half + 2):
+            t_rows = slice(c * two * V, (c + 1) * two * V)
+            row = 2 * c + iota((two, D), 0) // PLON
+            kept = (row != index[0]) & (row != index[1])
+            here = d_mixed[c * two : (c + 1) * two, :].astype(F32)
+            here = jnp.where(kept, here, 0.0).astype(BF16)
+            row = 2 * c + iota((HEADS, two * V), 1) // ROW
+            kept = (row != index[0]) & (row != index[1])
+            d_score = jnp.where(kept, d_probs[:, t_rows], 0.0)
+            token_back(c * two, probs[:, t_rows].astype(BF16), d_score, here)
+        return multiply(half * HALF, HALF, 15 + half)
+
+    send_grad[2].wait_recv()
+    agg_back(0)
+    stores = [half_back(0)]
+    send_grad[0].wait_recv()
+    send_grad[1].wait_recv()
     for copy in send_lay:
         copy.start()
-    h_lay[pl.ds(0, SIDE), :] = r_lay[pl.ds(HALF + EDGE, SIDE), :]
-    rows_of = from_quads()
-    cell_grad = jnp.concatenate(
-        [nn(rows_of, h_grad[0:HALF, :]), nn(rows_of, h_grad[HALF:N, :])], axis=0
-    ).astype(BF16)
-    d_mixed[...] = nt(cell_grad, w_out[...]).astype(BF16)
-    shape = (heads_here * GROUP, WIDE)
-    own_lanes = one_hot(iota(shape, 0) // GROUP == iota(shape, 1) // HD)
-    for g in range(N // GROUP):
-        rows, t_rows = slice(g * GROUP, (g + 1) * GROUP), slice(g * SPAN, (g + 1) * SPAN)
-        for n in range(D // WIDE):
-            cols = slice(n * WIDE, (n + 1) * WIDE)
-            spread = jnp.concatenate([d_mixed[rows, cols]] * heads_here, axis=0) * own_lanes
-            out = nt(spread, values[t_rows, cols])
-            for h in range(heads_here):
-                part = jnp.where(same_patch, out[h * GROUP : (h + 1) * GROUP], 0.0)
-                head = n * heads_here + h
-                d_probs[head : head + 1, t_rows] = jnp.sum(part, axis=0, keepdims=True)
-    prob, d_prob = stack(probs[...]), stack(d_probs[...])
-    d_score = unstack(prob * (d_prob - over_tokens(prob * d_prob, jnp.add)))
-    prob = probs[...]
-
-    loads["plan"].wait()
-    index = (plan[0, 0], plan[0, 1])
+    agg_back(1)
+
     shape = (PLON, N)
     for k, name in enumerate(index):
         start = jnp.where(name >= 0, name * PLON, -N)
@@ -351,21 +393,14 @@
         row = jnp.zeros((2 * HEADS, ROW), F32)
         for r in range(PLAT):
             lanes = slice(r * ROW, (r + 1) * ROW)
-            here = jnp.concatenate([prob[:, lanes], d_score[:, lanes]], axis=0)
+            here = jnp.concatenate([probs[:, lanes], d_probs[:, lanes]], axis=0)
             row = jnp.where(name == r, here, row)
         pad = jnp.zeros((2 * HEADS, WIDE - ROW), F32)
         move_out_p[k] = jnp.concatenate([row, pad], axis=1).astype(BF16)
         send_move[k].start()
         send_move[2 + k].start()
 
-    spot = iota((HEADS, N * V), 1) // ROW
-    probs_ref[:, 0 : N * V] = prob.astype(BF16)
-    kept = (spot != index[0]) & (spot != index[1])
-    scores_ref[:, 0 : N * V] = jnp.where(kept, d_score, 0.0).astype(BF16)
-    spot = iota((N, D), 0) // PLON
-    kept = (spot != index[0]) & (spot != index[1])
-    mixdot_ref[0:N, :] = jnp.where(kept, d_mixed[...].astype(F32), 0.0).astype(BF16)
-
+    stores.append(half_back(1))
     for copy in send_lay:
         copy.wait_recv()
     for half in (0, 1):
@@ -374,32 +409,15 @@
     for copy in send_move:
         copy.wait_recv()
     arrived = [move_in[k].astype(F32)[:PLON] for k in range(2)]
-    mixdot_ref[N : N + 2 * PLON, :] = jnp.concatenate(arrived, axis=0).astype(BF16)
+    here = jnp.concatenate(arrived, axis=0).astype(BF16)
     arrived = [move_in_p[k].astype(F32)[:, :ROW] for k in range(2)]
-    arrived = jnp.concatenate(arrived, axis=1).astype(BF16)
-    probs_ref[:, N * V :] = arrived[:HEADS]
-    scores_ref[:, N * V :] = arrived[HEADS:]
+    arrived = jnp.concatenate(arrived, axis=1)
+    token_back(N, arrived[:HEADS].astype(BF16), arrived[HEADS:], here)
+    stores.append(multiply(N, two, 17))
+    for store in stores:
+        store.wait()
     for copy in send_cot + send_cell + send_lay + send_grad + send_move:
         copy.wait_send()
-
-
-def back(mixdot_ref, probs_ref, scores_ref, value_ref, kq_ref, lay_ref, grad_ref, lay_out_ref, d_values):
-    @pl.when(pl.program_id(0) == 0)
-    def _():
-        lay_out_ref[...] = lay_ref[...]
-
-    patches, tokens = mixdot_ref.shape[0], probs_ref.shape[1]
-    expand = one_hot(iota((tokens, patches), 0) // V == iota((tokens, patches), 1))
-    heads = head_rows()
-    for n in range(D // WIDE):
-        cols = slice(n * WIDE, (n + 1) * WIDE)
-        wide = tn(probs_ref[...], heads[:, cols]) * nn(expand, mixdot_ref[:, cols])
-        d_values[:, cols] = wide.astype(BF16)
-    twice = jnp.concatenate([scores_ref[...]] * 2, axis=0)
-    for n in range(D // WIDE):
-        cols = slice(n * WIDE, (n + 1) * WIDE)
-        out = nt(d_values[...], value_ref[cols, :]) + tn(twice, kq_ref[:, cols])
-        grad_ref[:, cols] = out.astype(BF16)
 
 
 def body(
@@ -411,41 +429,39 @@
     vmem = pl.BlockSpec(memory_space=pltpu.VMEM)
     weight = pltpu.VMEM((D, D), BF16)
     patch = pltpu.VMEM((N, D), BF16)
-    tokens = (PLAT + 2) * ROW
-    lay, mixdot, probs, scores, kq = pl.pallas_call(
-        functools.partial(front, n_lat, n_lon),
+    layer_out, token_grad = pl.pallas_call(
+        functools.partial(layer, n_lat, n_lon),
         out_shape=(
             jax.ShapeDtypeStruct((N, D), BF16),
-            jax.ShapeDtypeStruct((N + 2 * PLON, D), BF16),
-            jax.ShapeDtypeStruct((HEADS, tokens), BF16),
-            jax.ShapeDtypeStruct((HEADS, tokens), BF16),
-            jax.ShapeDtypeStruct((2 * HEADS, D), BF16),
+            jax.ShapeDtypeStruct((TOKENS, D), BF16),
         ),
         in_specs=[hbm] * 14,
-        out_specs=(vmem,) * 5,
+        out_specs=(vmem, hbm),
         scratch_shapes=[pltpu.VMEM((N * V, D), BF16)]
-        + [weight] * 7
+        + [weight, pltpu.VMEM((D, DEEP), BF16)]
+        + [weight] * 5
         + [patch]
         + [pltpu.VMEM((PLAT, 2, PLON), jnp.int32)] * 2
         + [pltpu.VMEM((D,), BF16)] * 2
         + [pltpu.SMEM((1, 2), jnp.int32)]
-        + [pltpu.VMEM((N * V, D), BF16)]
+        + [pltpu.VMEM((N * V, D), BF16), pltpu.VMEM((TOKENS, DEEP), BF16)]
+        + [pltpu.VMEM((TOKENS, D), BF16)]
         + [pltpu.VMEM((HEADS, N * V), F32)] * 2
         + [patch] * 2
-        + [pltpu.VMEM((HEADS, N * V), F32)]
+        + [pltpu.VMEM((HEADS, N * V), F32), pltpu.VMEM((2 * HEADS, D), BF16)]
         + [patch] * 8
         + [patch] * 9
         + [pltpu.VMEM((2, 32, D), BF16)] * 2
         + [pltpu.VMEM((2, 2 * HEADS, WIDE), BF16)] * 2
         + [
-            pltpu.SemaphoreType.DMA((15,)),
+            pltpu.SemaphoreType.DMA((18,)),
             pltpu.SemaphoreType.DMA((16,)),
             pltpu.SemaphoreType.DMA((16,)),
         ],
         compiler_params=pltpu.CompilerParams(
-            collective_id=0, has_side_effects=True, vmem_limit_bytes=44 * 1024 * 1024
+            collective_id=0, has_side_effects=True, vmem_limit_bytes=56 * 1024 * 1024
         ),
-        name="front",
+        name="layer",
     )(
         var_tokens.reshape(N * V, D),
         jnp.transpose(ocean_mask, (0, 2, 1)),
@@ -457,28 +473,6 @@
         out_cotangent.reshape(N, D),
     )
 
-    two = 2 * PLON
-    fixed = lambda shape: pl.BlockSpec(shape, lambda r: (0,) * len(shape))
-    token_grad, layer_out = pl.pallas_call(
-        back,
-        grid=(PLAT // 2 + 1,),
-        out_shape=(
-            jax.ShapeDtypeStruct((tokens, D), BF16),
-            jax.ShapeDtypeStruct((N, D), BF16),
-        ),
-        in_specs=[
-            pl.BlockSpec((two, D), lambda r: (r, 0)),
-            pl.BlockSpec((HEADS, two * V), lambda r: (0, r)),
-            pl.BlockSpec((HEADS, two * V), lambda r: (0, r)),
-            fixed((D, D)),
-            fixed((2 * HEADS, D)),
-            fixed((N, D)),
-        ],
-        out_specs=(pl.BlockSpec((two * V, D), lambda r: (r, 0)), fixed((N, D))),
-        scratch_shapes=[pltpu.VMEM((two * V, D), BF16)],
-        compiler_params=pltpu.CompilerParams(vmem_limit_bytes=24 * 1024 * 1024),
-        name="back",
-    )(mixdot, probs, scores, agg_value, kq, lay)
     return (
         layer_out.reshape(PLAT, PLON, D),
         token_grad.reshape(PLAT + 2, PLON, V, D),

time: 68.4 us -> 57.7 us (0.84); the launches traced: 67.2 us -> 57.5 us
  Pallas kernels: 55.8 us -> 50.7 us
  local copies, waits for them, and re-layouts: 10.8 us -> 6.21 us
    pallas_call x2 -> x1, Pallas kernels: 55.8 us -> 50.7 us  [body(): pl.pallas_call(functools.partial(layer, n_lat, n_lon), out_shape=(jax.Sha...]
    unnamed x20 -> x2, local copies, waits for them, and re-layouts: 10.8 us -> 6.21 us
where the time goes in v2:
time: 57.7 us; the launch traced here: 57.5 us
  Pallas kernels  50.7 us (88%)
  local copies, waits for them, and re-layouts  6.21 us (11%)
  between operations  0.64 us (1%)
    pallas_call x1, Pallas kernels, body(): pl.pallas_call(functools.partial(layer, n_lat, n_lon), out_shape=(jax.Sha...  50.7 us
    unnamed x2, local copies, waits for them, and re-layouts  6.21 us

profile of v2, /device:TPU:6, one launch (start us, length us, event | category | flops | bytes accessed | tf_op | source)
XLA Modules:
  0.0 57.5 jit_solution(10113078115598608718)
XLA Ops:
  0.6 50.7 %layer.1 = (bf16[192,1024]{1,0:T(8,128)(2,1)}, bf16[1920,1024]{1,0:T(8,128)(2,1)}) custom-call(bf16[1536,1024]{1,0:T(8,128)(2,1)} %bitcast.8, s32[8,2,24]{2,1,0:T(2,128)} %bitcast.11, s32[8,2,24]{2,1,0:T(2,128)} %bitcast.12, s32[1,2]{1,0:T(1,128)} %bitcast.13, bf16[1024]{0:T(1024)(128)(2,1)} %query_hbm.1, bf16[1024]{0:T(1024)(128)(2,1)} %gain_hbm.1, ...), custom_call_target="tpu_custom_call" | custom-call | tf_op jit(solution)/shard_map/layer/pallas_call | solution.py:432
  51.3 1.8 %copy.18 = bf16[8,24,1024]{2,1,0:T(8,128)(2,1)} copy(bf16[8,24,1024]{2,1,0:T(8,128)(2,1)} %bitcast.9) | data formatting | bytes 786432
  53.1 4.4 %copy.19 = bf16[10,24,8,1024]{3,2,1,0:T(8,128)(2,1)} copy(bf16[10,24,8,1024]{3,2,1,0:T(8,128)(2,1)} %bitcast.7) | data formatting | bytes 7864320

commit v3 on v2

--- a/solution.py
+++ b/solution.py
@@ -88,10 +88,10 @@
     n_lat, n_lon,
     tok_hbm, ocean_hbm, land_hbm, plan_hbm, query_hbm, gain_hbm,
     key_hbm, value_hbm, out_hbm, wq_hbm, wk_hbm, wv_hbm, wo_hbm, cot_hbm,
-    lay_ref, grad_hbm,
+    lay_ref, grad_out,
     tok, w_key, w_value, w_out, w_q, w_k, w_v, w_o, cot,
     ocean, land, query, gain, plan,
-    values, d_values, grad_out, probs, d_probs, mixed, d_mixed, live, kq,
+    values, d_values, probs, d_probs, mixed, d_mixed, live, kq,
     h_cot, h_cell, h_lay, h_grad, r_cot, r_cell, r_lay, r_grad,
     normed, b_q, b_k, b_v, b_mixdot, b_mix, d_q, d_k, d_v,
     move_out, move_in, move_out_p, move_in_p,
@@ -107,23 +107,25 @@
         return pltpu.make_async_copy(src, dst, load_sem.at[slot])
 
     upper, lower = pl.ds(0, HALF * V), pl.ds(HALF * V, HALF * V)
-    loads = {
-        "tok1": load(tok_hbm.at[lower], tok.at[lower], 0),
-        "value": load(value_hbm, w_value.at[:, pl.ds(0, D)], 1),
-        "key": load(key_hbm, w_key, 2),
-        "query": load(query_hbm, query, 3),
-        "cot": load(cot_hbm, cot, 4),
-        "ocean": load(ocean_hbm, ocean, 5),
-        "land": load(land_hbm, land, 6),
-        "tok0": load(tok_hbm.at[upper], tok.at[upper], 7),
-        "out": load(out_hbm, w_out, 8),
-        "wo": load(wo_hbm, w_o, 9),
-        "gain": load(gain_hbm, gain, 10),
-        "plan": load(plan_hbm, plan, 11),
-        "wq": load(wq_hbm, w_q, 12),
-        "wk": load(wk_hbm, w_k, 13),
-        "wv": load(wv_hbm, w_v, 14),
+    parts = {
+        "tok1": (tok_hbm.at[lower], tok.at[lower]),
+        "value": (value_hbm, w_value.at[:, pl.ds(0, D)]),
+        "key": (key_hbm, w_key),
+        "query": (query_hbm, query),
+        "ocean": (ocean_hbm, ocean),
+        "land": (land_hbm, land),
+        "cot": (cot_hbm, cot),
+        "tok0": (tok_hbm.at[upper], tok.at[upper]),
+        "out": (out_hbm, w_out),
+        "wo": (wo_hbm, w_o),
+        "wq": (wq_hbm, w_q),
+        "wk": (wk_hbm, w_k),
+        "wv": (wv_hbm, w_v),
+        "gain": (gain_hbm, gain),
+        "plan": (plan_hbm, plan),
     }
+    loads = {name: load(*ends, k) for k, (name, ends) in enumerate(parts.items())}
+
     early = ("tok1", "value", "key", "query", "cot", "ocean", "land")
     for name in early:
         loads[name].start()
@@ -162,6 +164,38 @@
         send(move_out_p.at[0], move_in_p.at[0], to_e, 14),
         send(move_out_p.at[1], move_in_p.at[1], to_w, 15),
     ]
+
+    loads["tok1"].wait()
+    loads["value"].wait()
+    for name in loads:
+        if name not in early:
+            loads[name].start()
+
+    def project_values(half):
+        t_rows = slice(half * HALF * V, (half + 1) * HALF * V)
+        for n in range(D // WIDE):
+            cols = slice(n * WIDE, (n + 1) * WIDE)
+            values[t_rows, cols] = nn(tok[t_rows, :], w_value[:, cols]).astype(BF16)
+
+    project_values(1)
+
+    loads["cot"].wait()
+    quads = to_quads()
+    for half in (1, 0):
+        rows = pl.ds(half * HALF, HALF)
+        h_cot[rows, :] = nn(quads, cot[rows, :]).astype(BF16)
+    r_cot[pl.ds(HALF + EDGE, SIDE), :] = h_cot[pl.ds(0, SIDE), :]
+    pl.semaphore_wait(barrier, 6)
+    for copy in send_cot:
+        copy.start()
+
+    loads["key"].wait()
+    loads["query"].wait()
+    picked = head_rows() * query[...][None, :]
+    key_query = nt(picked, w_key[...]) * (1.0 / HD**0.5)
+    high = key_query.astype(BF16)
+    low = key_query - high.astype(F32)
+    kq[...] = jnp.concatenate([high.astype(F32), low], axis=0).astype(BF16)
 
     loads["ocean"].wait()
     loads["land"].wait()
@@ -175,32 +209,6 @@
     there = nn(jnp.ones((HEADS, 32), F32), jnp.where(mine, there, 0.0))
     live[...] = jnp.where(iota((HEADS, N * V), 1) % V < 4, 1.0, there)
 
-    loads["cot"].wait()
-    quads = to_quads()
-    for half in (1, 0):
-        rows = pl.ds(half * HALF, HALF)
-        h_cot[rows, :] = nn(quads, cot[rows, :]).astype(BF16)
-    r_cot[pl.ds(HALF + EDGE, SIDE), :] = h_cot[pl.ds(0, SIDE), :]
-
-    loads["key"].wait()
-    loads["query"].wait()
-    picked = head_rows() * query[...][None, :]
-    key_query = nt(picked, w_key[...]) * (1.0 / HD**0.5)
-    high = key_query.astype(BF16)
-    low = key_query - high.astype(F32)
-    both = jnp.concatenate([high.astype(F32), low, jnp.zeros((LANES - 2 * HEADS, D), F32)], axis=0)
-    kq[...] = both[: 2 * HEADS].astype(BF16)
-    w_value[:, D:DEEP] = both.T.astype(BF16)
-
-    loads["tok1"].wait()
-    loads["value"].wait()
-    for name in loads:
-        if name not in early:
-            loads[name].start()
-    pl.semaphore_wait(barrier, 6)
-    for copy in send_cot:
-        copy.start()
-
     shape = (GROUP, SPAN)
     same_patch = iota(shape, 0) == iota(shape, 1) // V
     lane_head = iota(shape, 1) // HD
@@ -210,6 +218,7 @@
         t_rows = slice(half * HALF * V, (half + 1) * HALF * V)
         if not half:
             loads["tok0"].wait()
+            project_values(0)
         both = nt(kq[...], tok[t_rows, :])
         scores = stack(both[:HEADS] + both[HEADS:])
         scores = jnp.where(stack(live[:, t_rows]) > 0.5, scores, -1e30)
@@ -218,8 +227,7 @@
         probs[:, t_rows] = prob
         for n in range(D // WIDE):
             cols = slice(n * WIDE, (n + 1) * WIDE)
-            vals = nn(tok[t_rows, :], w_value[:, cols]).astype(BF16)
-            values[t_rows, cols] = vals
+            vals = values[t_rows, cols]
             for g in range(HALF // GROUP):
                 span = slice(g * SPAN, (g + 1) * SPAN)
                 weigh = [
@@ -248,6 +256,9 @@
         copy.wait_recv()
     loads["wo"].wait()
     b_mixdot[...] = nt(r_cot[...], w_o[...]).astype(BF16)
+
+    deep = jnp.concatenate([kq[...].astype(F32), jnp.zeros((LANES - 2 * HEADS, D), F32)], axis=0)
+    w_value[:, D:DEEP] = deep.T.astype(BF16)
 
     for copy in send_cell:
         copy.wait_recv()
@@ -353,14 +364,11 @@
         pad = jnp.zeros((LANES - 2 * HEADS, two * V), F32)
         d_values[t_rows, D:DEEP] = jnp.concatenate([d_score, d_score, pad], axis=0).T.astype(BF16)
 
-    def multiply(first, count, slot):
+    def multiply(first, count):
         t_rows = pl.ds(first * V, count * V)
         for n in range(D // WIDE):
             cols = slice(n * WIDE, (n + 1) * WIDE)
             grad_out[t_rows, cols] = nt(d_values[t_rows, :], w_value[cols, :]).astype(BF16)
-        store = pltpu.make_async_copy(grad_out.at[t_rows], grad_hbm.at[t_rows], load_sem.at[slot])
-        store.start()
-        return store
 
     def half_back(half):
         for c in range(2 * half, 2 * half + 2):
@@ -373,11 +381,11 @@
             kept = (row != index[0]) & (row != index[1])
             d_score = jnp.where(kept, d_probs[:, t_rows], 0.0)
             token_back(c * two, probs[:, t_rows].astype(BF16), d_score, here)
-        return multiply(half * HALF, HALF, 15 + half)
+        multiply(half * HALF, HALF)
 
     send_grad[2].wait_recv()
     agg_back(0)
-    stores = [half_back(0)]
+    half_back(0)
     send_grad[0].wait_recv()
     send_grad[1].wait_recv()
     for copy in send_lay:
@@ -400,7 +408,7 @@
         send_move[k].start()
         send_move[2 + k].start()
 
-    stores.append(half_back(1))
+    half_back(1)
     for copy in send_lay:
         copy.wait_recv()
     for half in (0, 1):
@@ -413,9 +421,7 @@
     arrived = [move_in_p[k].astype(F32)[:, :ROW] for k in range(2)]
     arrived = jnp.concatenate(arrived, axis=1)
     token_back(N, arrived[:HEADS].astype(BF16), arrived[HEADS:], here)
-    stores.append(multiply(N, two, 17))
-    for store in stores:
-        store.wait()
+    multiply(N, two)
     for copy in send_cot + send_cell + send_lay + send_grad + send_move:
         copy.wait_send()
 
@@ -431,12 +437,9 @@
     patch = pltpu.VMEM((N, D), BF16)
     layer_out, token_grad = pl.pallas_call(
         functools.partial(layer, n_lat, n_lon),
-        out_shape=(
-            jax.ShapeDtypeStruct((N, D), BF16),
-            jax.ShapeDtypeStruct((TOKENS, D), BF16),
-        ),
+        out_shape=(pltpu.VMEM((N, D), BF16), pltpu.VMEM((TOKENS, D), BF16)),
         in_specs=[hbm] * 14,
-        out_specs=(vmem, hbm),
+        out_specs=(vmem, vmem),
         scratch_shapes=[pltpu.VMEM((N * V, D), BF16)]
         + [weight, pltpu.VMEM((D, DEEP), BF16)]
         + [weight] * 5
@@ -445,7 +448,6 @@
         + [pltpu.VMEM((D,), BF16)] * 2
         + [pltpu.SMEM((1, 2), jnp.int32)]
         + [pltpu.VMEM((N * V, D), BF16), pltpu.VMEM((TOKENS, DEEP), BF16)]
-        + [pltpu.VMEM((TOKENS, D), BF16)]
         + [pltpu.VMEM((HEADS, N * V), F32)] * 2
         + [patch] * 2
         + [pltpu.VMEM((HEADS, N * V), F32), pltpu.VMEM((2 * HEADS, D), BF16)]
@@ -454,7 +456,7 @@
         + [pltpu.VMEM((2, 32, D), BF16)] * 2
         + [pltpu.VMEM((2, 2 * HEADS, WIDE), BF16)] * 2
         + [
-            pltpu.SemaphoreType.DMA((18,)),
+            pltpu.SemaphoreType.DMA((15,)),
             pltpu.SemaphoreType.DMA((16,)),
             pltpu.SemaphoreType.DMA((16,)),
         ],

time: 57.7 us -> 51.4 us (0.89)
  local copies, waits for them, and re-layouts: 6.21 us -> 2.67 us
  Pallas kernels: 50.7 us -> 48 us
    unnamed x2, local copies, waits for them, and re-layouts: 6.21 us -> 2.67 us
    pallas_call x1, Pallas kernels: 50.7 us -> 48 us  [body(): pl.pallas_call(functools.partial(layer, n_lat, n_lon), out_shape=(pltpu.V...]
where the time goes in v3:
time: 51.4 us; the launch traced here: 51.3 us
  Pallas kernels  48 us (93%)
  local copies, waits for them, and re-layouts  2.67 us (5%)
  between operations  0.64 us (1%)
    pallas_call x1, Pallas kernels, body(): pl.pallas_call(functools.partial(layer, n_lat, n_lon), out_shape=(pltpu.V...  48 us
    unnamed x2, local copies, waits for them, and re-layouts  2.67 us

profile of v3, /device:TPU:6, one launch (start us, length us, event | category | flops | bytes accessed | tf_op | source)
XLA Modules:
  0.0 51.3 jit_solution(6131711555016233457)
XLA Ops:
  0.6 48.0 %layer.1 = (bf16[192,1024]{1,0:T(8,128)(2,1)S(1)}, bf16[1920,1024]{1,0:T(8,128)(2,1)S(1)}) custom-call(bf16[1536,1024]{1,0:T(8,128)(2,1)} %bitcast.9, s32[8,2,24]{2,1,0:T(2,128)} %bitcast.11, s32[8,2,24]{2,1,0:T(2,128)} %bitcast.12, s32[1,2]{1,0:T(1,128)} %bitcast.13, bf16[1024]{0:T(1024)(128)(2,1)} %query_hbm.1, bf16[1024]{0:T(1024)(128)(2,1)} %gain_hbm.1, ...), custom_call_target="tpu_custom_call" | custom-call | tf_op jit(solution)/shard_map/layer/pallas_call | solution.py:438
  48.7 0.7 %copy.18 = bf16[8,24,1024]{2,1,0:T(8,128)(2,1)} copy(bf16[8,24,1024]{2,1,0:T(8,128)(2,1)S(1)} %bitcast.8) | data formatting | bytes 786432
  49.4 1.9 %copy.19 = bf16[10,24,8,1024]{3,2,1,0:T(8,128)(2,1)} copy(bf16[10,24,8,1024]{3,2,1,0:T(8,128)(2,1)S(1)} %bitcast.7) | data formatting | bytes 7864320

commit v4 on v3

--- a/solution.py
+++ b/solution.py
@@ -126,7 +126,7 @@
     }
     loads = {name: load(*ends, k) for k, (name, ends) in enumerate(parts.items())}
 
-    early = ("tok1", "value", "key", "query", "cot", "ocean", "land")
+    early = ("cot", "tok1", "value", "key", "query", "ocean", "land")
     for name in early:
         loads[name].start()
 
@@ -165,29 +165,30 @@
         send(move_out_p.at[1], move_in_p.at[1], to_w, 15),
     ]
 
-    loads["tok1"].wait()
-    loads["value"].wait()
-    for name in loads:
-        if name not in early:
-            loads[name].start()
-
-    def project_values(half):
-        t_rows = slice(half * HALF * V, (half + 1) * HALF * V)
-        for n in range(D // WIDE):
-            cols = slice(n * WIDE, (n + 1) * WIDE)
-            values[t_rows, cols] = nn(tok[t_rows, :], w_value[:, cols]).astype(BF16)
-
-    project_values(1)
-
     loads["cot"].wait()
     quads = to_quads()
     for half in (1, 0):
         rows = pl.ds(half * HALF, HALF)
         h_cot[rows, :] = nn(quads, cot[rows, :]).astype(BF16)
     r_cot[pl.ds(HALF + EDGE, SIDE), :] = h_cot[pl.ds(0, SIDE), :]
+
+    loads["tok1"].wait()
+    loads["value"].wait()
+    for name in loads:
+        if name not in early:
+            loads[name].start()
+
+    def project_values(half, blocks=range(D // WIDE)):
+        t_rows = slice(half * HALF * V, (half + 1) * HALF * V)
+        for n in blocks:
+            cols = slice(n * WIDE, (n + 1) * WIDE)
+            values[t_rows, cols] = nn(tok[t_rows, :], w_value[:, cols]).astype(BF16)
+
+    project_values(1, range(1))
     pl.semaphore_wait(barrier, 6)
     for copy in send_cot:
         copy.start()
+    project_values(1, range(1, D // WIDE))
 
     loads["key"].wait()
     loads["query"].wait()
@@ -287,33 +288,40 @@
             out = jnp.where(win_head == h, x[h * patches : (h + 1) * patches], out)
         return out
 
+    wins = range(N // patches)
     for g in range(D // WIDE):
         cols = slice(g * WIDE, (g + 1) * WIDE)
-        for w in range(N // patches):
-            upper, lower = pl.ds(w * half_win, half_win), pl.ds(HALF + w * half_win, half_win)
-
-            def get(ref):
-                return jnp.concatenate([ref[upper, cols], ref[lower, cols]], axis=0)
-
-            def put(ref, x):
-                x = x.astype(BF16)
-                ref[upper, cols] = x[:half_win]
-                ref[lower, cols] = x[half_win:]
-
-            keys, vals = get(b_k), get(b_v)
-            queries = per_head(get(b_q))
-            scores = nt(keys, queries) * (1.0 / HD**0.5) + bias
-            expo = jnp.exp(scores - jnp.max(scores, axis=0, keepdims=True))
-            prob = expo / jnp.sum(expo, axis=0, keepdims=True)
-            prob_b = prob.astype(BF16)
-            put(b_mix, own_blocks(tn(prob_b, vals)))
-            mixdot = per_head(get(b_mixdot))
-            d_prob = nt(vals, mixdot)
-            inner = jnp.sum(d_prob * prob, axis=0, keepdims=True)
-            d_score = (prob * (d_prob - inner) * (1.0 / HD**0.5)).astype(BF16)
-            put(d_v, nn(prob_b, mixdot))
-            put(d_k, nn(d_score, queries))
-            put(d_q, own_blocks(tn(d_score, keys)))
+
+        def get(ref, w):
+            upper = ref[w * half_win : (w + 1) * half_win, cols]
+            lower = ref[HALF + w * half_win : HALF + (w + 1) * half_win, cols]
+            return jnp.concatenate([upper, lower], axis=0)
+
+        def put(ref, w, x):
+            x = x.astype(BF16)
+            ref[w * half_win : (w + 1) * half_win, cols] = x[:half_win]
+            ref[HALF + w * half_win : HALF + (w + 1) * half_win, cols] = x[half_win:]
+
+        keys, vals = [get(b_k, w) for w in wins], [get(b_v, w) for w in wins]
+        queries = [per_head(get(b_q, w)) for w in wins]
+        scores = [nt(keys[w], queries[w]) * (1.0 / HD**0.5) + bias for w in wins]
+        mixdot = [per_head(get(b_mixdot, w)) for w in wins]
+        d_prob = [nt(vals[w], mixdot[w]) for w in wins]
+        expo = [jnp.exp(scores[w] - jnp.max(scores[w], axis=0, keepdims=True)) for w in wins]
+        prob = [expo[w] / jnp.sum(expo[w], axis=0, keepdims=True) for w in wins]
+        prob_b = [prob[w].astype(BF16) for w in wins]
+        for w in wins:
+            put(d_v, w, nn(prob_b[w], mixdot[w]))
+        inner = [jnp.sum(d_prob[w] * prob[w], axis=0, keepdims=True) for w in wins]
+        d_score = [
+            (prob[w] * (d_prob[w] - inner[w]) * (1.0 / HD**0.5)).astype(BF16) for w in wins
+        ]
+        for w in wins:
+            put(b_mix, w, own_blocks(tn(prob_b[w], vals[w])))
+        for w in wins:
+            put(d_k, w, nn(d_score[w], queries[w]))
+        for w in wins:
+            put(d_q, w, own_blocks(tn(d_score[w], keys[w])))
 
     d_norm = nt(d_q[...], w_q[...]) + nt(d_k[...], w_k[...]) + nt(d_v[...], w_v[...])
     wide = r_cell[...].astype(F32)
@@ -386,10 +394,10 @@
     send_grad[2].wait_recv()
     agg_back(0)
     half_back(0)
+    for copy in send_lay:
+        copy.start()
     send_grad[0].wait_recv()
     send_grad[1].wait_recv()
-    for copy in send_lay:
-        copy.start()
     agg_back(1)
 
     shape = (PLON, N)
@@ -409,11 +417,6 @@
         send_move[2 + k].start()
 
     half_back(1)
-    for copy in send_lay:
-        copy.wait_recv()
-    for half in (0, 1):
-        rows = slice(half * HALF, (half + 1) * HALF)
-        lay_ref[rows, :] = nn(rows_of, h_lay[rows, :]).astype(BF16)
     for copy in send_move:
         copy.wait_recv()
     arrived = [move_in[k].astype(F32)[:PLON] for k in range(2)]
@@ -422,6 +425,11 @@
     arrived = jnp.concatenate(arrived, axis=1)
     token_back(N, arrived[:HEADS].astype(BF16), arrived[HEADS:], here)
     multiply(N, two)
+    for copy in send_lay:
+        copy.wait_recv()
+    for half in (0, 1):
+        rows = slice(half * HALF, (half + 1) * HALF)
+        lay_ref[rows, :] = nn(rows_of, h_lay[rows, :]).astype(BF16)
     for copy in send_cot + send_cell + send_lay + send_grad + send_move:
         copy.wait_send()
 

time: 51.4 us -> 47.3 us (0.920)
  Pallas kernels: 48 us -> 43.9 us
    pallas_call x1, Pallas kernels: 48 us -> 43.9 us  [body(): pl.pallas_call(functools.partial(layer, n_lat, n_lon), out_shape=(pltpu.V...]
where the time goes in v4:
time: 47.3 us; the launch traced here: 47.2 us
  Pallas kernels  43.9 us (93%)
  local copies, waits for them, and re-layouts  2.67 us (6%)
  between operations  0.64 us (1%)
    pallas_call x1, Pallas kernels, body(): pl.pallas_call(functools.partial(layer, n_lat, n_lon), out_shape=(pltpu.V...  43.9 us
    unnamed x2, local copies, waits for them, and re-layouts  2.67 us

profile of v4, /device:TPU:6, one launch (start us, length us, event | category | flops | bytes accessed | tf_op | source)
XLA Modules:
  0.0 47.2 jit_solution(18173493078098812743)
XLA Ops:
  0.6 43.9 %layer.1 = (bf16[192,1024]{1,0:T(8,128)(2,1)S(1)}, bf16[1920,1024]{1,0:T(8,128)(2,1)S(1)}) custom-call(bf16[1536,1024]{1,0:T(8,128)(2,1)} %bitcast.9, s32[8,2,24]{2,1,0:T(2,128)} %bitcast.11, s32[8,2,24]{2,1,0:T(2,128)} %bitcast.12, s32[1,2]{1,0:T(1,128)} %bitcast.13, bf16[1024]{0:T(1024)(128)(2,1)} %query_hbm.1, bf16[1024]{0:T(1024)(128)(2,1)} %gain_hbm.1, ...), custom_call_target="tpu_custom_call" | custom-call | tf_op jit(solution)/shard_map/layer/pallas_call | solution.py:446
  44.6 0.7 %copy.18 = bf16[8,24,1024]{2,1,0:T(8,128)(2,1)} copy(bf16[8,24,1024]{2,1,0:T(8,128)(2,1)S(1)} %bitcast.8) | data formatting | bytes 786432
  45.3 1.9 %copy.19 = bf16[10,24,8,1024]{3,2,1,0:T(8,128)(2,1)} copy(bf16[10,24,8,1024]{3,2,1,0:T(8,128)(2,1)S(1)} %bitcast.7) | data formatting | bytes 7864320

commit v5 on v4

--- a/solution.py
+++ b/solution.py
@@ -393,9 +393,9 @@
 
     send_grad[2].wait_recv()
     agg_back(0)
-    half_back(0)
     for copy in send_lay:
         copy.start()
+    half_back(0)
     send_grad[0].wait_recv()
     send_grad[1].wait_recv()
     agg_back(1)

time: 47.3 us -> 48 us (1.015)
  the two profiles are of different devices: /device:TPU:6 before, /device:TPU:22 now
where the time goes in v5:
time: 48 us; the launch traced here: 47.9 us
  Pallas kernels  44.6 us (93%)
  local copies, waits for them, and re-layouts  2.67 us (6%)
  between operations  0.64 us (1%)
    pallas_call x1, Pallas kernels, body(): pl.pallas_call(functools.partial(layer, n_lat, n_lon), out_shape=(pltpu.V...  44.6 us
    unnamed x2, local copies, waits for them, and re-layouts  2.67 us

profile of v5, /device:TPU:22, one launch (start us, length us, event | category | flops | bytes accessed | tf_op | source)
XLA Modules:
  0.0 47.9 jit_solution(9874703896659983450)
XLA Ops:
  0.6 44.6 %layer.1 = (bf16[192,1024]{1,0:T(8,128)(2,1)S(1)}, bf16[1920,1024]{1,0:T(8,128)(2,1)S(1)}) custom-call(bf16[1536,1024]{1,0:T(8,128)(2,1)} %bitcast.9, s32[8,2,24]{2,1,0:T(2,128)} %bitcast.11, s32[8,2,24]{2,1,0:T(2,128)} %bitcast.12, s32[1,2]{1,0:T(1,128)} %bitcast.13, bf16[1024]{0:T(1024)(128)(2,1)} %query_hbm.1, bf16[1024]{0:T(1024)(128)(2,1)} %gain_hbm.1, ...), custom_call_target="tpu_custom_call" | custom-call | tf_op jit(solution)/shard_map/layer/pallas_call | solution.py:446
  45.2 0.7 %copy.18 = bf16[8,24,1024]{2,1,0:T(8,128)(2,1)} copy(bf16[8,24,1024]{2,1,0:T(8,128)(2,1)S(1)} %bitcast.8) | data formatting | bytes 786432
  46.0 1.9 %copy.19 = bf16[10,24,8,1024]{3,2,1,0:T(8,128)(2,1)} copy(bf16[10,24,8,1024]{3,2,1,0:T(8,128)(2,1)S(1)} %bitcast.7) | data formatting | bytes 7864320

commit v6 on v5

--- a/solution.py
+++ b/solution.py
@@ -393,8 +393,6 @@
 
     send_grad[2].wait_recv()
     agg_back(0)
-    for copy in send_lay:
-        copy.start()
     half_back(0)
     send_grad[0].wait_recv()
     send_grad[1].wait_recv()
@@ -415,6 +413,8 @@
         move_out_p[k] = jnp.concatenate([row, pad], axis=1).astype(BF16)
         send_move[k].start()
         send_move[2 + k].start()
+    for copy in send_lay:
+        copy.start()
 
     half_back(1)
     for copy in send_move:

time: 48 us -> 48.2 us (level)
  the two profiles are of different devices: /device:TPU:22 before, /device:TPU:14 now
where the time goes in v6:
time: 48.2 us; the launch traced here: 48.1 us
  Pallas kernels  44.8 us (93%)
  local copies, waits for them, and re-layouts  2.67 us (6%)
  between operations  0.64 us (1%)
    pallas_call x1, Pallas kernels, body(): pl.pallas_call(functools.partial(layer, n_lat, n_lon), out_shape=(pltpu.V...  44.8 us
    unnamed x2, local copies, waits for them, and re-layouts  2.67 us

profile of v6, /device:TPU:14, one launch (start us, length us, event | category | flops | bytes accessed | tf_op | source)
XLA Modules:
  0.0 48.1 jit_solution(11441943950447806780)
XLA Ops:
  0.6 44.8 %layer.1 = (bf16[192,1024]{1,0:T(8,128)(2,1)S(1)}, bf16[1920,1024]{1,0:T(8,128)(2,1)S(1)}) custom-call(bf16[1536,1024]{1,0:T(8,128)(2,1)} %bitcast.9, s32[8,2,24]{2,1,0:T(2,128)} %bitcast.11, s32[8,2,24]{2,1,0:T(2,128)} %bitcast.12, s32[1,2]{1,0:T(1,128)} %bitcast.13, bf16[1024]{0:T(1024)(128)(2,1)} %query_hbm.1, bf16[1024]{0:T(1024)(128)(2,1)} %gain_hbm.1, ...), custom_call_target="tpu_custom_call" | custom-call | tf_op jit(solution)/shard_map/layer/pallas_call | solution.py:446
  45.4 0.7 %copy.18 = bf16[8,24,1024]{2,1,0:T(8,128)(2,1)} copy(bf16[8,24,1024]{2,1,0:T(8,128)(2,1)S(1)} %bitcast.8) | data formatting | bytes 786432
  46.1 1.9 %copy.19 = bf16[10,24,8,1024]{3,2,1,0:T(8,128)(2,1)} copy(bf16[10,24,8,1024]{3,2,1,0:T(8,128)(2,1)S(1)} %bitcast.7) | data formatting | bytes 7864320
